TPU v7x, 32 devices: a whole 2x2x4 slice. The times are simulated.
32 devices in a mesh: gx: 8 (over z, y), gy: 4 (over x, core).
Axes of the slice: x: 2, y: 2, z: 4, core: 2. Of those that a mesh axis runs over, the one named last changes fastest.
Arguments:
- flux_perturbation: float32 [2, 4096, 4096], P(None, 'gx', 'gy'), may hold values from -6 to 6
- archived_nominal_heat_levels: float32 [2, 2, 4096, 4096], P(None, None, 'gx', 'gy'), may hold values from -4 to 4
- archived_solidity_labels: int32 [2, 2, 4096, 4096], P(None, None, 'gx', 'gy'), may hold values from 0 to 2
Outputs:
- hess_vec: float32 [2, 4096, 4096], P(None, 'gx', 'gy')
Inputs may be any that keep to these rules, and one draw needn't show every extreme that they name: `archived_solidity_labels`: 0 is solid, 1 mushy, 2 liquid.
All inputs are finite; a program needn't handle non-finite values.
Results may differ from a plain program's by a relative error of at most 0.000061.
Values sent between devices are 32-bit elements; how exact they have to be, the bound alone decides.
A program may use at most 192 MiB of HBM per device.

v0:
```python
import math

import jax
import jax.numpy as jnp
import numpy as np
from jax import lax
from jax.experimental import pallas as pl
from jax.experimental.pallas import tpu as pltpu
from jax.sharding import PartitionSpec as P

TIME_STEP = 0.1
OBS_WEIGHT = 10.0
PRIOR_GAIN = 0.005
HIGHEST = lax.Precision.HIGHEST


def with_halo(cells, sides, width):
    for axis, dim in sides:
        count = lax.axis_size(axis)
        ends = count - 1
        head = lax.slice_in_dim(cells, 0, width, axis=dim)
        tail = lax.slice_in_dim(cells, cells.shape[dim] - width, cells.shape[dim], axis=dim)
        cells = jnp.concatenate(
            [
                lax.ppermute(tail, axis, [(i, (i + 1) % count) for i in range(ends)]),
                cells,
                lax.ppermute(head, axis, [((i + 1) % count, i) for i in range(ends)]),
            ],
            axis=dim,
        )
    return cells


def surface_rim(field):
    padded = with_halo(field, (("gx", 1), ("gy", 2)), 1)
    return padded[:, 2:, 1:-1] + padded[:, :-2, 1:-1] + padded[:, 1:-1, 2:] + padded[:, 1:-1, :-2]


def cos_sin(horizontal_line_total, col_count, modulus):
    row_ids = jnp.arange(horizontal_line_total, dtype=jnp.int32)[:, None]
    col_ids = jnp.arange(col_count, dtype=jnp.int32)[None, :]
    angles = (row_ids * col_ids % modulus).astype(jnp.float32) * (2.0 * math.pi / modulus)
    return (jnp.cos(angles), jnp.sin(angles))


def tables(length):
    bit_count = length.bit_length() - 1
    outer_len = 2 ** (bit_count // 2)
    inner_len = length // outer_len
    cos_outer, sin_outer = cos_sin(outer_len, outer_len, outer_len)
    cos_inner, sin_inner = cos_sin(inner_len, inner_len, inner_len)
    twist_cos, twist_sin = cos_sin(outer_len, inner_len, length)
    outer_fwd = jnp.stack([cos_outer, -sin_outer])
    inner_fwd = jnp.stack([jnp.stack([cos_inner, -sin_inner]), jnp.stack([sin_inner, cos_inner])])
    inner_inv = jnp.stack([jnp.stack([cos_inner, sin_inner]), jnp.stack([-sin_inner, cos_inner])])
    outer_inv = jnp.stack([cos_outer, -sin_outer])
    freq_index = (
        jnp.arange(outer_len, dtype=jnp.int32)[:, None]
        + outer_len * jnp.arange(inner_len, dtype=jnp.int32)[None, :]
    )
    signed = jnp.where(freq_index < length // 2, freq_index, freq_index - length).astype(
        jnp.float32
    )
    wave_sq = (signed * (2.0 * math.pi / length)) ** 2
    return (
        length,
        outer_len,
        inner_len,
        outer_fwd,
        inner_fwd,
        inner_inv,
        outer_inv,
        twist_cos,
        twist_sin,
        wave_sq,
    )


def forward(field, table):
    (
        length,
        outer_len,
        inner_len,
        outer_fwd,
        inner_fwd,
        inner_inv,
        outer_inv,
        twist_cos,
        twist_sin,
        wave_sq,
    ) = table
    grid = field.reshape(field.shape[:-1] + (outer_len, inner_len))
    stepped = jnp.einsum("...ab,rak->...rkb", grid, outer_fwd, precision=HIGHEST)
    step_re = stepped[..., 0, :, :]
    step_im = stepped[..., 1, :, :]
    twisted = jnp.stack(
        [step_re * twist_cos + step_im * twist_sin, step_im * twist_cos - step_re * twist_sin],
        axis=-3,
    )
    spec = jnp.einsum("...rkb,rsbm->...skm", twisted, inner_fwd, precision=HIGHEST)
    return (spec[..., 0, :, :], spec[..., 1, :, :])


def inverse(spec_re, spec_im, table):
    (
        length,
        outer_len,
        inner_len,
        outer_fwd,
        inner_fwd,
        inner_inv,
        outer_inv,
        twist_cos,
        twist_sin,
        wave_sq,
    ) = table
    stacked = jnp.stack([spec_re, spec_im], axis=-3)
    halved = jnp.einsum("...skm,srbm->...rkb", stacked, inner_inv, precision=HIGHEST)
    half_re = halved[..., 0, :, :]
    half_im = halved[..., 1, :, :]
    turned = jnp.stack(
        [half_re * twist_cos - half_im * twist_sin, half_im * twist_cos + half_re * twist_sin],
        axis=-3,
    )
    grid = jnp.einsum("...rkb,rka->...ab", turned, outer_inv, precision=HIGHEST)
    return grid.reshape(grid.shape[:-2] + (length,)) / length


def shards_general(flux_perturbation, archived_nominal_heat_levels, archived_solidity_labels):
    capacity = jnp.where(
        archived_solidity_labels == 0, 1.0, jnp.where(archived_solidity_labels == 1, 4.0, 1.25)
    ).astype(jnp.float32)
    diffusion_advance = jnp.where(
        archived_solidity_labels == 0, 1.0, jnp.where(archived_solidity_labels == 1, 0.6, 0.35)
    ).astype(jnp.float32)
    diffusion_advance = diffusion_advance * (1.0 + 0.5 * jnp.tanh(archived_nominal_heat_levels))
    rows = lax.all_to_all(flux_perturbation, "gx", split_axis=2, concat_axis=1, tiled=True)
    row_table = tables(rows.shape[1])
    first_u = TIME_STEP * flux_perturbation / capacity[0, 0]
    second_top = TIME_STEP * flux_perturbation + TIME_STEP * (
        diffusion_advance[0, 0] * (surface_rim(first_u) - 6.0 * first_u) + flux_perturbation
    )
    second_low = TIME_STEP * diffusion_advance[0, 1] * first_u
    top_u = second_top / capacity[1, 0]
    low_u = second_low / capacity[1, 1]
    third_top = second_top + TIME_STEP * (
        diffusion_advance[1, 0] * (surface_rim(top_u) - 6.0 * top_u + low_u) + flux_perturbation
    )
    misfit = OBS_WEIGHT * third_top / capacity[1, 0]
    adj_three = misfit / capacity[1, 0]
    push_top = TIME_STEP * diffusion_advance[1, 0] * adj_three
    adj_two_top = adj_three + (surface_rim(push_top) - 6.0 * push_top) / capacity[1, 0]
    adj_two_low = push_top / capacity[1, 1]
    pull_top = TIME_STEP * diffusion_advance[0, 0] * adj_two_top
    pull_low = TIME_STEP * diffusion_advance[0, 1] * adj_two_low
    adj_one_top = adj_two_top + (surface_rim(pull_top) - 6.0 * pull_top + pull_low) / capacity[0, 0]
    data_term = TIME_STEP * (adj_three + adj_two_top + adj_one_top)
    row_re, row_im = forward(jnp.swapaxes(rows, 1, 2), row_table)
    wave_x = row_table[-1]
    second_x = jnp.swapaxes(
        inverse(2.0 * PRIOR_GAIN * wave_x * row_re, 2.0 * PRIOR_GAIN * wave_x * row_im, row_table),
        1,
        2,
    )
    fourth_x = jnp.swapaxes(
        inverse(
            PRIOR_GAIN * wave_x * wave_x * row_re, PRIOR_GAIN * wave_x * wave_x * row_im, row_table
        ),
        1,
        2,
    )
    second_back, fourth_part = (
        lax.all_to_all(second_x, "gx", split_axis=1, concat_axis=2, tiled=True),
        lax.all_to_all(fourth_x, "gx", split_axis=1, concat_axis=2, tiled=True),
    )
    cols_dir, cols_second = (
        lax.all_to_all(flux_perturbation, "gy", split_axis=1, concat_axis=2, tiled=True),
        lax.all_to_all(second_back, "gy", split_axis=1, concat_axis=2, tiled=True),
    )
    col_table = tables(cols_dir.shape[2])
    dir_re, dir_im = forward(cols_dir, col_table)
    sec_re, sec_im = forward(cols_second, col_table)
    wave_y = col_table[-1]
    mixed = inverse(
        PRIOR_GAIN * wave_y * wave_y * dir_re + wave_y * sec_re,
        PRIOR_GAIN * wave_y * wave_y * dir_im + wave_y * sec_im,
        col_table,
    )
    mixed_back = lax.all_to_all(mixed, "gy", split_axis=2, concat_axis=1, tiled=True)
    return data_term + fourth_part + mixed_back


OUTER = 16


def half_spectrum(xs):
    n = len(xs)
    if n == 2:
        return [(xs[0] + xs[1], None), (xs[0] - xs[1], None)]
    even, odd = half_spectrum(xs[0::2]), half_spectrum(xs[1::2])
    out = [None] * (n // 2 + 1)
    for k in range(n // 4 + 1):
        er, ei = even[k]
        orr, oi = odd[k]
        if k == 0:
            out[0] = (er + orr, None)
            out[n // 2] = (er - orr, None)
        elif k == n // 4:
            out[k] = (er, -orr)
        else:
            c, s = math.cos(2 * math.pi * k / n), math.sin(2 * math.pi * k / n)
            if 8 * k == n:
                tr, ti = c * (orr + oi), c * (oi - orr)
            else:
                tr, ti = c * orr + s * oi, c * oi - s * orr
            out[k] = (er + tr, ei + ti)
            out[n // 2 - k] = (er - tr, ti - ei)
    return out


def half_spectrum_t(gs):
    half = len(gs) - 1
    n = 2 * half
    if n == 2:
        return [gs[0][0] + gs[1][0], gs[0][0] - gs[1][0]]
    even, odd = [], []
    for m in range(n // 4 + 1):
        gr, gi = gs[m]
        if m == 0:
            hr = gs[half][0]
            even.append((gr + hr, None))
            odd.append((gr - hr, None))
        elif m == n // 4:
            even.append((gr, None))
            odd.append((-gi, None))
        else:
            hr, hi = gs[half - m]
            even.append((gr + hr, gi - hi))
            dr, di = gr - hr, gi + hi
            c, s = math.cos(2 * math.pi * m / n), math.sin(2 * math.pi * m / n)
            if 8 * m == n:
                odd.append((c * (dr - di), c * (dr + di)))
            else:
                odd.append((c * dr - s * di, c * di + s * dr))
    out = [None] * n
    out[0::2] = half_spectrum_t(even)
    out[1::2] = half_spectrum_t(odd)
    return out


def line_tables(length):
    inner = length // OUTER
    groups = OUTER // 2
    b = np.arange(inner)[:, None]
    mats = np.zeros((groups, 2 * inner, 2 * inner))
    freq = np.zeros((groups, 2 * inner), np.int64)
    scale = math.sqrt(2.0 / length)
    for k1 in range(1, groups):
        k = k1 + OUTER * np.arange(inner)
        angle = 2.0 * math.pi * ((b * k[None, :]) % length) / length
        c, s = np.cos(angle) * scale, np.sin(angle) * scale
        mats[k1 - 1] = np.block([[c, -s], [s, c]])
        freq[k1 - 1] = np.concatenate([k, k])
    last = groups - 1
    for part, first in ((0, 0), (1, groups)):
        k = first + OUTER * np.arange(inner // 2)
        angle = 2.0 * math.pi * ((b * k[None, :]) % length) / length
        c, s = np.cos(angle) * scale, np.sin(angle) * scale
        k_sin = k.copy()
        if first == 0:
            c[:, 0] = math.sqrt(1.0 / length)
            k_sin[0] = length // 2
            s[:, 0] = -math.sqrt(1.0 / length) * (1 - 2 * (np.arange(inner) % 2))
        span = slice(part * inner, (part + 1) * inner)
        mats[last][span, span] = np.concatenate([c, -s], axis=1)
        freq[last][span] = np.concatenate([k, k_sin])
    signed = np.where(freq < length // 2, freq, freq - length)
    wave = (signed * (2.0 * math.pi / length)) ** 2
    return mats, wave


def two_parts(mats):
    top = np.asarray(mats, np.float32).astype(jnp.bfloat16)
    rest = (np.asarray(mats, np.float64) - top.astype(np.float64)).astype(jnp.bfloat16)
    return top, rest


def split(x):
    top = x.astype(jnp.bfloat16)
    return top, (x - top.astype(jnp.float32)).astype(jnp.bfloat16)


def dot32(a, b):
    return jnp.dot(a, b, preferred_element_type=jnp.float32)


def right(x, hi, lo):
    top, rest = split(x)
    return dot32(top, hi) + (dot32(rest, hi) + dot32(top, lo))


def left(hi, lo, x):
    top, rest = split(x)
    return dot32(hi, top) + (dot32(lo, top) + dot32(hi, rest))


def pairs(spec):
    ends = len(spec) - 1
    return [spec[k] for k in range(1, ends)] + [(spec[0][0], spec[ends][0])]


def unpairs(groups):
    return [(groups[-1][0], None)] + groups[:-1] + [(groups[-1][1], None)]


def y_forward(x_ref, hi_ref, lo_ref, out_ref):
    parts, wide = x_ref.shape[0], x_ref.shape[-1]
    inner = parts * wide // OUTER
    per = wide // inner
    xs = [x_ref[a // per, 0, :, (a % per) * inner : (a % per + 1) * inner] for a in range(OUTER)]
    width = out_ref.shape[-1]
    each = 2 * inner // width
    for g, (re, im) in enumerate(pairs(half_spectrum(xs))):
        res = right(jnp.concatenate([re, im], axis=1), hi_ref[g], lo_ref[g])
        for c in range(each):
            out_ref[g * each + c, 0] = res[:, c * width : (c + 1) * width]


def y_inverse(x_ref, hi_ref, lo_ref, out_ref):
    parts, wide = out_ref.shape[0], out_ref.shape[-1]
    inner = parts * wide // OUTER
    per = wide // inner
    width = x_ref.shape[-1]
    each = 2 * inner // width
    groups = []
    for g in range(OUTER // 2):
        spec = jnp.concatenate([x_ref[g * each + c, 0] for c in range(each)], axis=1)
        res = right(spec, hi_ref[g], lo_ref[g])
        groups.append((res[:, :inner], res[:, inner:]))
    for a, slab in enumerate(half_spectrum_t(unpairs(groups))):
        out_ref[a // per, 0, :, (a % per) * inner : (a % per + 1) * inner] = slab


def x_apply(x_ref, ky_ref, kx_ref, fhi_ref, flo_ref, ihi_ref, ilo_ref, out_ref):
    count, nvec, rows, width = x_ref.shape
    inner = count * rows // OUTER
    per = inner // rows

    def slab(a):
        return jnp.concatenate(
            [x_ref[a * per : (a + 1) * per, v].reshape(inner, width) for v in range(nvec)], axis=1
        )

    ky = jnp.concatenate([ky_ref[...]] * nvec, axis=1)
    groups = []
    for g, (re, im) in enumerate(pairs(half_spectrum([slab(a) for a in range(OUTER)]))):
        spec = left(fhi_ref[g], flo_ref[g], jnp.concatenate([re, im], axis=0))
        wave = kx_ref[g] + ky
        res = left(ihi_ref[g], ilo_ref[g], PRIOR_GAIN * wave * wave * spec)
        groups.append((res[:inner], res[inner:]))
    for a, res in enumerate(half_spectrum_t(unpairs(groups))):
        for v in range(nvec):
            out_ref[a * per : (a + 1) * per, v] = res[:, v * width : (v + 1) * width].reshape(
                per, rows, width
            )


def cost(flops, moved):
    return pl.CostEstimate(flops=int(flops), bytes_accessed=int(moved), transcendentals=0)


def prior(q, heat, labels):
    across, along = lax.axis_size("gx"), lax.axis_size("gy")
    nvec, bx, by = q.shape
    length = by * along
    count = across * along
    rows = bx // along
    width = length // count
    mats, wave = line_tables(length)
    fhi, flo = two_parts(mats)
    thi, tlo = two_parts(np.swapaxes(mats, 1, 2))
    params = pltpu.CompilerParams(vmem_limit_bytes=VMEM_BYTES)
    lines_shape = jax.ShapeDtypeStruct((along, 1, rows, by), jnp.float32)
    packed_shape = jax.ShapeDtypeStruct((count, 1, rows, width), jnp.float32)
    work = 6 * mats.size * bx * by // length
    moved = 8 * bx * by + 4 * mats.size

    me = lax.axis_index("gx") * along + lax.axis_index("gy")
    ky = lax.dynamic_slice_in_dim(
        jnp.asarray(wave.reshape(1, length), jnp.float32), me * width, width, axis=1
    )
    kx = jnp.asarray(wave[:, :, None], jnp.float32)
    turns = range(nvec)
    starts = [q[v] for v in turns]
    starts[-1], *rim = lax.optimization_barrier((starts[-1], *rim_rows(q, heat, labels)))
    whole_y = [
        lax.all_to_all(starts[v].reshape(along, 1, rows, by), "gy", 0, 0, tiled=True) for v in turns
    ]
    spec_y = [
        pl.pallas_call(
            y_forward, out_shape=packed_shape, compiler_params=params, name="y_forward",
            cost_estimate=cost(work, moved),
        )(whole_y[v], fhi, flo)
        for v in turns
    ]
    side = rim_sides(q, heat, labels, *rim)
    spec_y[-1], side = lax.optimization_barrier((spec_y[-1], side))
    whole_x = [lax.all_to_all(spec_y[v], ("gx", "gy"), 0, 0, tiled=True) for v in turns]
    done_x = [
        pl.pallas_call(
            x_apply, out_shape=packed_shape, compiler_params=params, name="x_apply",
            cost_estimate=cost(4 * work, 2 * moved),
        )(whole_x[v], ky, kx, thi, tlo, fhi, flo)
        for v in turns
    ]
    done_x[-1], side = lax.optimization_barrier((done_x[-1], side))
    data = data_part(q, heat, labels, *rim, side)
    back_y = [lax.all_to_all(done_x[v], ("gx", "gy"), 0, 0, tiled=True) for v in turns]
    back_y[0], data = lax.optimization_barrier((back_y[0], data))
    done_y = [
        pl.pallas_call(
            y_inverse, out_shape=lines_shape, compiler_params=params, name="y_inverse",
            cost_estimate=cost(work, moved),
        )(back_y[v], thi, tlo)
        for v in turns
    ]
    back = [lax.all_to_all(done_y[v], "gy", 0, 0, tiled=True) for v in turns]
    return [back[v].reshape(bx, by) for v in turns], data


RIM = 8
VMEM_BYTES = 58 * 2**20


def shift(axis, step):
    count = lax.axis_size(axis)
    return [(i, i + step) for i in range(count) if 0 <= i + step < count]


def near(q, heat, labels, cut):
    first = cut(q)
    return jnp.concatenate(
        [
            first,
            (cut(labels) + 1).astype(jnp.float32).reshape((-1,) + first.shape[1:]),
            cut(heat).reshape((-1,) + first.shape[1:])[:-1],
        ]
    )


def rim_rows(q, heat, labels):
    bx = q.shape[1]
    above = lax.ppermute(
        near(q, heat, labels, lambda f: f[..., bx - RIM :, :]), "gx", shift("gx", 1)
    )
    below = lax.ppermute(near(q, heat, labels, lambda f: f[..., :RIM, :]), "gx", shift("gx", -1))
    return above, below


def rim_sides(q, heat, labels, above, below):
    by = q.shape[2]
    ends = []
    for cols, step in ((slice(0, RIM), -1), (slice(by - RIM, by), 1)):
        line = jnp.concatenate(
            [above[..., cols], near(q, heat, labels, lambda f: f[..., cols]), below[..., cols]],
            axis=1,
        )
        ends.append(lax.ppermute(jnp.swapaxes(line, 1, 2), "gy", shift("gy", step)))
    gap = jnp.zeros((ends[0].shape[0], 128 - 2 * RIM, ends[0].shape[2]), jnp.float32)
    return jnp.swapaxes(jnp.concatenate([ends[0], gap, ends[1]], axis=1), 1, 2)


def data_strips(q_ref, heat_ref, labels_ref, above_ref, below_ref, side_ref, out_ref, f_ref):
    nvec, bx, by = out_ref.shape
    f_ref[:, :RIM, :by] = above_ref[...]
    f_ref[:, RIM + bx :, :by] = below_ref[...]
    f_ref[:, :, by:] = side_ref[...]
    levels_at = nvec + 4
    for v in range(nvec):
        f_ref[v, RIM : RIM + bx, :by] = q_ref[v]
    for i in range(4):
        f_ref[nvec + i, RIM : RIM + bx, :by] = (labels_ref[i // 2, i % 2] + 1).astype(jnp.float32)
    for i in range(3):
        f_ref[levels_at + i, RIM : RIM + bx, :by] = heat_ref[i]
    strip = 32
    tall, wide = strip + 2 * RIM, f_ref.shape[2]

    def rim(f):
        return (pltpu.roll(f, 1, 0) + pltpu.roll(f, tall - 1, 0)) + (
            pltpu.roll(f, 1, 1) + pltpu.roll(f, wide - 1, 1)
        )

    def one(s, carry):
        first = pl.multiple_of(s * strip, strip)
        field = lambda i: f_ref[i, pl.ds(first, tall), :]

        def inverse_capacity(label):
            return jnp.where(label == 2.0, 0.25, jnp.where(label == 3.0, 0.8, 1.0))

        def conduct(label, level):
            base = jnp.where(
                label == 1.0, 1.0, jnp.where(label == 2.0, 0.6, jnp.where(label == 3.0, 0.35, 0.0))
            )
            return TIME_STEP * base * (1.0 + 0.5 * jnp.tanh(level))

        label = [field(nvec + i) for i in range(4)]
        ic_top0, ic_top1 = inverse_capacity(label[0]), inverse_capacity(label[2])
        ic_low1 = inverse_capacity(label[3])
        c_top0 = conduct(label[0], field(nvec + 4))
        c_low0 = conduct(label[1], field(nvec + 5))
        c_top1 = conduct(label[2], field(nvec + 6))
        for v in range(nvec):
            q = field(v)
            first_u = TIME_STEP * q * ic_top0
            second_top = (2.0 * TIME_STEP) * q + c_top0 * (rim(first_u) - 6.0 * first_u)
            top_u = second_top * ic_top1
            low_u = c_low0 * first_u * ic_low1
            third_top = (
                second_top + c_top1 * (rim(top_u) - 6.0 * top_u + low_u) + TIME_STEP * q
            )
            adj_three = OBS_WEIGHT * third_top * ic_top1 * ic_top1
            push_top = c_top1 * adj_three
            adj_two = adj_three + (rim(push_top) - 6.0 * push_top) * ic_top1
            pull_top = c_top0 * adj_two
            pull_low = c_low0 * (push_top * ic_low1)
            adj_one = adj_two + (rim(pull_top) - 6.0 * pull_top + pull_low) * ic_top0
            total = TIME_STEP * (adj_three + adj_two + adj_one)
            out_ref[v, pl.ds(first, strip), :] = total[RIM : RIM + strip, :by]
        return carry

    lax.fori_loop(0, bx // strip, one, 0)


def data_part(q, heat, labels, above, below, side):
    nvec, bx, by = q.shape
    levels = heat.reshape(-1, bx, by)
    whole = lambda x: pl.BlockSpec(x.shape, lambda i: (0,) * x.ndim)
    return pl.pallas_call(
        data_strips,
        grid=(1,),
        in_specs=[
            whole(q), pl.BlockSpec((3, bx, by), lambda i: (0, 0, 0)), whole(labels),
            whole(above), whole(below), whole(side),
        ],
        out_specs=whole(q),
        out_shape=jax.ShapeDtypeStruct(q.shape, jnp.float32),
        scratch_shapes=[pltpu.VMEM((nvec + 7, bx + 2 * RIM, by + 128), jnp.float32)],
        compiler_params=pltpu.CompilerParams(vmem_limit_bytes=VMEM_BYTES),
        cost_estimate=cost(400 * q.size, 24 * q.size),
        name="data_strips",
    )(q, levels, labels, above, below, side)


def shards(q, heat, labels):
    nvec, bx, by = q.shape
    along, across = lax.axis_size("gy"), lax.axis_size("gx")
    rows, width = bx // along, by // across
    square = bx * across == by * along
    if not square or rows % 16 or width % 128 or by % (by * along // OUTER) or bx % 32:
        return shards_general(q, heat, labels)
    parts, data = prior(q, heat, labels)
    return jnp.stack([data[v] + part for v, part in enumerate(parts)])


def solution(mesh):
    in_specs = (P(None, "gx", "gy"), P(None, None, "gx", "gy"), P(None, None, "gx", "gy"))
    out_specs = P(None, "gx", "gy")
    return jax.shard_map(shards, mesh=mesh, in_specs=in_specs, out_specs=out_specs, check_vma=False)
```

profile of v0, /device:TPU:13, one launch (start us, length us, event | category | flops | bytes accessed | tf_op | source)
XLA Modules:
  0.0 342.0 jit_solution(15168943003384914818)
XLA Ops:
  0.0 4.8 %fusion.3 = (f32[1,512,1024]{2,1,0:T(8,128)}, f32[512,1024]{1,0:T(8,128)}) fusion(f32[2,512,1024]{2,1,0:T(8,128)} %q_ref.1), kind=kLoop, calls=%fused_computation.17 | loop fusion | bytes 8388608 | tf_op jit(solution)/shard_map/slice | solution.py:394
  4.8 4.3 %all-to-all-start = ((f32[4,1,128,1024]{3,2,1,0:T(8,128)}), f32[4,1,128,1024]{3,2,1,0:T(8,128)S(1)}, u32[]{:S(2)}, u32[]{:S(2)}) async-start(f32[4,1,128,1024]{3,2,1,0:T(8,128)} %bitcast.23), calls=%async_computation | async-start | bytes 4194304 | tf_op jit(solution)/shard_map/all_to_all | solution.py:397
  9.1 1.0 fusion.2
  10.1 0.9 fusion.5
  11.0 1.0 add_convert_fusion
  12.0 3.1 collective-permute-start
  15.2 2.1 collective-permute-start.1
  17.3 11.5 %collective-permute-done.above_ref = f32[9,8,1024]{2,1,0:T(8,128)S(1)} collective-permute-done((f32[9,8,1024]{2,1,0:T(8,128)S(1)}, f32[9,8,1024]{2,1,0:T(8,128)S(1)}, u32[]{:S(2)}, u32[]{:S(2)}) %collective-permute-start) | collective-permute-done | bytes 294944 | tf_op jit(solution)/shard_map/ppermute | solution.py:453
  28.8 5.1 %all-to-all-done.x_ref = f32[4,1,128,1024]{3,2,1,0:T(8,128)S(1)} async-done(((f32[4,1,128,1024]{3,2,1,0:T(8,128)}), f32[4,1,128,1024]{3,2,1,0:T(8,128)S(1)}, u32[]{:S(2)}, u32[]{:S(2)}) %all-to-all-start) | async-done | bytes 2097184 | tf_op jit(solution)/shard_map/all_to_all | solution.py:397
  33.9 1.3 copy-done.1
  35.2 4.4 %all-to-all-start.3 = ((f32[4,1,128,1024]{3,2,1,0:T(8,128)}), f32[4,1,128,1024]{3,2,1,0:T(8,128)S(1)}, u32[]{:S(2)}, u32[]{:S(2)}) async-start(f32[4,1,128,1024]{3,2,1,0:T(8,128)} %bitcast.22), calls=%async_computation.3 | async-start | bytes 4194304 | tf_op jit(solution)/shard_map/all_to_all | solution.py:397
  39.7 7.5 %y_forward.2 = f32[32,1,128,128]{3,2,1,0:T(8,128)} custom-call(f32[4,1,128,1024]{3,2,1,0:T(8,128)} %copy-done.1, bf16[8,512,512]{2,1,0:T(8,128)(2,1)} %constant.36.clone.hi_ref.ihi_ref, bf16[8,512,512]{2,1,0:T(8,128)(2,1)} %constant.37.clone.lo_ref.ilo_ref), custom_call_target="tpu_custom_call" | custom-call | flops 1610612736 | bytes 12582912 | tf_op jit(solution)/shard_map/y_forward/pallas_call | solution.py:400
  47.2 17.3 %all-to-all-done.3.x_ref = f32[4,1,128,1024]{3,2,1,0:T(8,128)S(1)} async-done(((f32[4,1,128,1024]{3,2,1,0:T(8,128)}), f32[4,1,128,1024]{3,2,1,0:T(8,128)S(1)}, u32[]{:S(2)}, u32[]{:S(2)}) %all-to-all-start.3) | async-done | bytes 2097184 | tf_op jit(solution)/shard_map/all_to_all | solution.py:397
  64.5 5.6 %all-to-all-start.1 = ((f32[32,1,128,128]{3,2,1,0:T(8,128)}), f32[32,1,128,128]{3,2,1,0:T(8,128)}, u32[]{:S(2)}, u32[]{:S(2)}) async-start(f32[32,1,128,128]{3,2,1,0:T(8,128)} %y_forward.2), calls=%async_computation.1 | async-start | bytes 4194304 | tf_op jit(solution)/shard_map/all_to_all | solution.py:408
  70.2 1.4 fusion.4
  71.9 1.9 fusion.1
  73.8 0.3 copy.24
  74.1 0.3 copy.29
  74.4 1.9 fusion
  76.6 0.3 copy.37
  77.0 0.9 fusion.6
  78.3 3.3 collective-permute-start.3
  81.8 1.9 collective-permute-start.2
  83.8 1.6 collective-permute-done.3
  85.4 0.7 copy.33
  86.0 2.9 collective-permute-done.2
  88.9 2.1 copy.32
  91.0 3.8 %maximum_bitcast_fusion.side_ref = f32[9,528,128]{2,1,0:T(8,128)} fusion(f32[9,8,528]{1,2,0:T(8,128)S(1)} %copy.33, f32[9,8,528]{1,2,0:T(8,128)} %copy.32, f32[128]{0:T(128)S(1)} %pad.3.clone), kind=kLoop, calls=%fused_computation.1 | loop fusion | flops 1216512 | bytes 2737664 | tf_op jit(solution)/shard_map/transpose | solution.py:470
  94.9 7.5 %y_forward.3 = f32[32,1,128,128]{3,2,1,0:T(8,128)} custom-call(f32[4,1,128,1024]{3,2,1,0:T(8,128)} %copy-done, bf16[8,512,512]{2,1,0:T(8,128)(2,1)} %constant.36.clone.hi_ref.ihi_ref, bf16[8,512,512]{2,1,0:T(8,128)(2,1)} %constant.37.clone.lo_ref.ilo_ref), custom_call_target="tpu_custom_call" | custom-call | flops 1610612736 | bytes 12582912 | tf_op jit(solution)/shard_map/y_forward/pallas_call | solution.py:400
  102.4 13.3 %all-to-all-done.1.x_ref = f32[32,1,128,128]{3,2,1,0:T(8,128)} async-done(((f32[32,1,128,128]{3,2,1,0:T(8,128)}), f32[32,1,128,128]{3,2,1,0:T(8,128)}, u32[]{:S(2)}, u32[]{:S(2)}) %all-to-all-start.1) | async-done | bytes 2097184 | tf_op jit(solution)/shard_map/all_to_all | solution.py:408
  115.7 7.4 %all-to-all-start.4 = ((f32[32,1,128,128]{3,2,1,0:T(8,128)}), f32[32,1,128,128]{3,2,1,0:T(8,128)S(1)}, u32[]{:S(2)}, u32[]{:S(2)}) async-start(f32[32,1,128,128]{3,2,1,0:T(8,128)} %y_forward.3), calls=%async_computation.4 | async-start | bytes 4194304 | tf_op jit(solution)/shard_map/all_to_all | solution.py:408
  123.1 1.2 constant_dynamic-slice_fusion.ky_ref
  124.4 16.3 %x_apply.2 = f32[32,1,128,128]{3,2,1,0:T(8,128)} custom-call(f32[32,1,128,128]{3,2,1,0:T(8,128)} %all-to-all-done.1.x_ref, f32[1,128]{1,0:T(1,128)} %constant_dynamic-slice_fusion.ky_ref, f32[8,512,1]{2,1,0:T(8,128)} %constant.35.clone.kx_ref, bf16[8,512,512]{2,1,0:T(8,128)(2,1)} %constant.38.clone.fhi_ref.hi_ref, ...), custom_call_target="tpu_custom_call" | custom-call | flops 6442450944 | bytes 25165824 | tf_op jit(solution)/shard_map/x_apply/pallas_call | solution.py:410
  140.6 28.1 %all-to-all-done.4.x_ref = f32[32,1,128,128]{3,2,1,0:T(8,128)S(1)} async-done(((f32[32,1,128,128]{3,2,1,0:T(8,128)}), f32[32,1,128,128]{3,2,1,0:T(8,128)S(1)}, u32[]{:S(2)}, u32[]{:S(2)}) %all-to-all-start.4) | async-done | bytes 2097184 | tf_op jit(solution)/shard_map/all_to_all | solution.py:408
  168.7 1.3 copy-done.3
  170.1 7.3 %all-to-all-start.2 = ((f32[32,1,128,128]{3,2,1,0:T(8,128)}), f32[32,1,128,128]{3,2,1,0:T(8,128)S(1)}, u32[]{:S(2)}, u32[]{:S(2)}) async-start(f32[32,1,128,128]{3,2,1,0:T(8,128)} %x_apply.2), calls=%async_computation.2 | async-start | bytes 4194304 | tf_op jit(solution)/shard_map/all_to_all | solution.py:418
  177.4 16.3 %x_apply.3 = f32[32,1,128,128]{3,2,1,0:T(8,128)} custom-call(f32[32,1,128,128]{3,2,1,0:T(8,128)} %copy-done.3, f32[1,128]{1,0:T(1,128)} %constant_dynamic-slice_fusion.ky_ref, f32[8,512,1]{2,1,0:T(8,128)} %constant.35.clone.kx_ref, bf16[8,512,512]{2,1,0:T(8,128)(2,1)} %constant.38.clone.fhi_ref.hi_ref, bf16[8,512,512]{2,1,0:T(8,128)(2,1)} %constant.39.clone.flo_ref.lo_ref, ...), custom_call_target="tpu_custom_call" | custom-call | flops 6442450944 | bytes 25165824 | tf_op jit(solution)/shard_map/x_apply/pallas_call | solution.py:410
  193.7 29.3 %all-to-all-done.2.x_ref = f32[32,1,128,128]{3,2,1,0:T(8,128)S(1)} async-done(((f32[32,1,128,128]{3,2,1,0:T(8,128)}), f32[32,1,128,128]{3,2,1,0:T(8,128)S(1)}, u32[]{:S(2)}, u32[]{:S(2)}) %all-to-all-start.2) | async-done | bytes 2097184 | tf_op jit(solution)/shard_map/all_to_all | solution.py:418
  223.0 7.4 %all-to-all-start.6 = ((f32[32,1,128,128]{3,2,1,0:T(8,128)}), f32[32,1,128,128]{3,2,1,0:T(8,128)}, u32[]{:S(2)}, u32[]{:S(2)}) async-start(f32[32,1,128,128]{3,2,1,0:T(8,128)} %x_apply.3), calls=%async_computation.6 | async-start | bytes 4194304 | tf_op jit(solution)/shard_map/all_to_all | solution.py:418
  230.4 37.5 %data_strips.1 = f32[2,512,1024]{2,1,0:T(8,128)} custom-call(f32[2,512,1024]{2,1,0:T(8,128)} %q_ref.1, f32[4,512,1024]{2,1,0:T(8,128)} %bitcast.21, s32[2,2,512,1024]{3,2,1,0:T(8,128)} %labels_ref.1, f32[9,8,1024]{2,1,0:T(8,128)} %copy-done.4, f32[9,8,1024]{2,1,0:T(8,128)} %copy-done.5, f32[9,528,128]{2,1,0:T(8,128)} %maximum_bitcast_fusion.side_ref), custom_call_target="tpu_custom_call" | custom-call | flops 419430400 | bytes 25165824 | tf_op jit(solution)/shard_map/data_strips/pallas_call | solution.py:538
  267.8 7.6 %y_inverse.2 = f32[4,1,128,1024]{3,2,1,0:T(8,128)} custom-call(f32[32,1,128,128]{3,2,1,0:T(8,128)} %copy-done.2, bf16[8,512,512]{2,1,0:T(8,128)(2,1)} %constant.38.clone.fhi_ref.hi_ref, bf16[8,512,512]{2,1,0:T(8,128)(2,1)} %constant.39.clone.flo_ref.lo_ref), custom_call_target="tpu_custom_call" | custom-call | flops 1610612736 | bytes 12582912 | tf_op jit(solution)/shard_map/y_inverse/pallas_call | solution.py:421
  275.4 0.5 all-to-all-done.6.x_ref
  275.9 5.0 %all-to-all-start.5 = ((f32[4,1,128,1024]{3,2,1,0:T(8,128)}), f32[4,1,128,1024]{3,2,1,0:T(8,128)S(1)}, u32[]{:S(2)}, u32[]{:S(2)}) async-start(f32[4,1,128,1024]{3,2,1,0:T(8,128)} %y_inverse.2), calls=%async_computation.5 | async-start | bytes 4194304 | tf_op jit(solution)/shard_map/all_to_all | solution.py:427
  280.9 7.6 %y_inverse.3 = f32[4,1,128,1024]{3,2,1,0:T(8,128)} custom-call(f32[32,1,128,128]{3,2,1,0:T(8,128)} %all-to-all-done.6.x_ref, bf16[8,512,512]{2,1,0:T(8,128)(2,1)} %constant.38.clone.fhi_ref.hi_ref, bf16[8,512,512]{2,1,0:T(8,128)(2,1)} %constant.39.clone.flo_ref.lo_ref), custom_call_target="tpu_custom_call" | custom-call | flops 1610612736 | bytes 12582912 | tf_op jit(solution)/shard_map/y_inverse/pallas_call | solution.py:421
  288.5 17.2 %all-to-all-done.5 = f32[4,1,128,1024]{3,2,1,0:T(8,128)S(1)} async-done(((f32[4,1,128,1024]{3,2,1,0:T(8,128)}), f32[4,1,128,1024]{3,2,1,0:T(8,128)S(1)}, u32[]{:S(2)}, u32[]{:S(2)}) %all-to-all-start.5) | async-done | bytes 2097184 | tf_op jit(solution)/shard_map/all_to_all | solution.py:427
  305.7 5.3 %all-to-all-start.7 = ((f32[4,1,128,1024]{3,2,1,0:T(8,128)}), f32[4,1,128,1024]{3,2,1,0:T(8,128)}, u32[]{:S(2)}, u32[]{:S(2)}) async-start(f32[4,1,128,1024]{3,2,1,0:T(8,128)} %y_inverse.3), calls=%async_computation.7 | async-start | bytes 4194304 | tf_op jit(solution)/shard_map/all_to_all | solution.py:427
  311.0 24.9 %all-to-all-done.7 = f32[4,1,128,1024]{3,2,1,0:T(8,128)} async-done(((f32[4,1,128,1024]{3,2,1,0:T(8,128)}), f32[4,1,128,1024]{3,2,1,0:T(8,128)}, u32[]{:S(2)}, u32[]{:S(2)}) %all-to-all-start.7) | async-done | bytes 2097184 | tf_op jit(solution)/shard_map/all_to_all | solution.py:427
  336.0 6.0 %slice_add_fusion.1 = (f32[2,512,1024]{2,1,0:T(8,128)}, f32[2,512,1024]{2,1,0:T(8,128)}) fusion(f32[1,512,1024]{2,1,0:T(8,128)S(1)} %bitcast.24, f32[2,512,1024]{2,1,0:T(8,128)} %data_strips.1, f32[1,512,1024]{2,1,0:T(8,128)} %bitcast.16, f32[2,512,1024]{2,1,0:T(8,128)} %custom-call), kind=kLoop, output_to_operand_aliasing={{0}: (3, {}), {1}: (3, {})}, calls=%fused_computation.3 | loop fusion | flops 1048576 | bytes 12582912 | tf_op jit(solution)/shard_map/add | solution.py:562
  (31 shorter events, 1.4 us)
Async XLA Ops:
  4.8 29.1 %all-to-all-start = ((f32[4,1,128,1024]{3,2,1,0:T(8,128)}), f32[4,1,128,1024]{3,2,1,0:T(8,128)S(1)}, u32[]{:S(2)}, u32[]{:S(2)}) async-start(f32[4,1,128,1024]{3,2,1,0:T(8,128)} %bitcast.23), calls=%async_computation | async-start | bytes 4194304 | tf_op jit(solution)/shard_map/all_to_all | solution.py:397
  12.0 16.8 %collective-permute-start = (f32[9,8,1024]{2,1,0:T(8,128)S(1)}, f32[9,8,1024]{2,1,0:T(8,128)S(1)}, u32[]{:S(2)}, u32[]{:S(2)}) collective-permute-start(f32[9,8,1024]{2,1,0:T(8,128)S(1)} %pad_maximum_fusion.1), channel_id=1, source_target_pairs={{0,4},{4,8},{8,12},{12,16},{16,20},{20,24},{24,28},{1,5},{5,9},{9,... | collective-permute-start | bytes 884744 | tf_op jit(solution)/shard_map/ppermute | solution.py:453
  15.2 13.6 %collective-permute-start.1 = (f32[9,8,1024]{2,1,0:T(8,128)S(1)}, f32[9,8,1024]{2,1,0:T(8,128)S(1)}, u32[]{:S(2)}, u32[]{:S(2)}) collective-permute-start(f32[9,8,1024]{2,1,0:T(8,128)S(1)} %pad_maximum_fusion.2), channel_id=1, source_target_pairs={{4,0},{8,4},{12,8},{16,12},{20,16},{24,20},{28,24},{5,1},{9,5},{13... | collective-permute-start | bytes 884744 | tf_op jit(solution)/shard_map/ppermute | solution.py:456
  28.8 48.2 %copy-start.4 = (f32[9,8,1024]{2,1,0:T(8,128)}, f32[9,8,1024]{2,1,0:T(8,128)S(1)}, u32[]{:S(2)}) copy-start(f32[9,8,1024]{2,1,0:T(8,128)S(1)} %collective-permute-done.above_ref) | copy-start | bytes 884740
  28.8 18.4 %copy-start.5 = (f32[9,8,1024]{2,1,0:T(8,128)}, f32[9,8,1024]{2,1,0:T(8,128)S(1)}, u32[]{:S(2)}) copy-start(f32[9,8,1024]{2,1,0:T(8,128)S(1)} %collective-permute-done.1.below_ref) | copy-start | bytes 884740
  33.9 1.3 copy-start.1
  35.2 29.3 %all-to-all-start.3 = ((f32[4,1,128,1024]{3,2,1,0:T(8,128)}), f32[4,1,128,1024]{3,2,1,0:T(8,128)S(1)}, u32[]{:S(2)}, u32[]{:S(2)}) async-start(f32[4,1,128,1024]{3,2,1,0:T(8,128)} %bitcast.22), calls=%async_computation.3 | async-start | bytes 4194304 | tf_op jit(solution)/shard_map/all_to_all | solution.py:397
  64.5 7.1 %copy-start = (f32[4,1,128,1024]{3,2,1,0:T(8,128)}, f32[4,1,128,1024]{3,2,1,0:T(8,128)S(1)}, u32[]{:S(2)}) copy-start(f32[4,1,128,1024]{3,2,1,0:T(8,128)S(1)} %all-to-all-done.3.x_ref) | copy-start | bytes 6291460
  64.5 51.2 %all-to-all-start.1 = ((f32[32,1,128,128]{3,2,1,0:T(8,128)}), f32[32,1,128,128]{3,2,1,0:T(8,128)}, u32[]{:S(2)}, u32[]{:S(2)}) async-start(f32[32,1,128,128]{3,2,1,0:T(8,128)} %y_forward.2), calls=%async_computation.1 | async-start | bytes 4194304 | tf_op jit(solution)/shard_map/all_to_all | solution.py:408
  78.3 7.1 %collective-permute-start.3 = (f32[9,8,528]{2,1,0:T(8,128)S(1)}, f32[9,8,528]{2,1,0:T(8,128)S(1)}, u32[]{:S(2)}, u32[]{:S(2)}) collective-permute-start(f32[9,8,528]{2,1,0:T(8,128)S(1)} %maximum_bitcast_fusion.2), channel_id=1, source_target_pairs={{0,1},{1,2},{2,3},{4,5},{5,6},{6,7},{8,9},{9,10},{10,11},{12,13},{... | collective-permute-start | bytes 456200 | tf_op jit(solution)/shard_map/ppermute | solution.py:468
  81.8 7.1 %collective-permute-start.2 = (f32[9,8,528]{2,1,0:T(8,128)S(1)}, f32[9,8,528]{2,1,0:T(8,128)S(1)}, u32[]{:S(2)}, u32[]{:S(2)}) collective-permute-start(f32[9,8,528]{2,1,0:T(8,128)S(1)} %maximum_bitcast_fusion.1), channel_id=1, source_target_pairs={{1,0},{2,1},{3,2},{5,4},{6,5},{7,6},{9,8},{10,9},{11,10},{13,12},{... | collective-permute-start | bytes 456200 | tf_op jit(solution)/shard_map/ppermute | solution.py:468
  115.7 53.0 %all-to-all-start.4 = ((f32[32,1,128,128]{3,2,1,0:T(8,128)}), f32[32,1,128,128]{3,2,1,0:T(8,128)S(1)}, u32[]{:S(2)}, u32[]{:S(2)}) async-start(f32[32,1,128,128]{3,2,1,0:T(8,128)} %y_forward.3), calls=%async_computation.4 | async-start | bytes 4194304 | tf_op jit(solution)/shard_map/all_to_all | solution.py:408
  168.7 1.4 copy-start.3
  170.1 52.9 %all-to-all-start.2 = ((f32[32,1,128,128]{3,2,1,0:T(8,128)}), f32[32,1,128,128]{3,2,1,0:T(8,128)S(1)}, u32[]{:S(2)}, u32[]{:S(2)}) async-start(f32[32,1,128,128]{3,2,1,0:T(8,128)} %x_apply.2), calls=%async_computation.2 | async-start | bytes 4194304 | tf_op jit(solution)/shard_map/all_to_all | solution.py:418
  223.0 44.8 %copy-start.2 = (f32[32,1,128,128]{3,2,1,0:T(8,128)}, f32[32,1,128,128]{3,2,1,0:T(8,128)S(1)}, u32[]{:S(2)}) copy-start(f32[32,1,128,128]{3,2,1,0:T(8,128)S(1)} %all-to-all-done.2.x_ref) | copy-start | bytes 6291460
  223.0 52.9 %all-to-all-start.6 = ((f32[32,1,128,128]{3,2,1,0:T(8,128)}), f32[32,1,128,128]{3,2,1,0:T(8,128)}, u32[]{:S(2)}, u32[]{:S(2)}) async-start(f32[32,1,128,128]{3,2,1,0:T(8,128)} %x_apply.3), calls=%async_computation.6 | async-start | bytes 4194304 | tf_op jit(solution)/shard_map/all_to_all | solution.py:418
  275.9 29.8 %all-to-all-start.5 = ((f32[4,1,128,1024]{3,2,1,0:T(8,128)}), f32[4,1,128,1024]{3,2,1,0:T(8,128)S(1)}, u32[]{:S(2)}, u32[]{:S(2)}) async-start(f32[4,1,128,1024]{3,2,1,0:T(8,128)} %y_inverse.2), calls=%async_computation.5 | async-start | bytes 4194304 | tf_op jit(solution)/shard_map/all_to_all | solution.py:427
  305.7 30.2 %all-to-all-start.7 = ((f32[4,1,128,1024]{3,2,1,0:T(8,128)}), f32[4,1,128,1024]{3,2,1,0:T(8,128)}, u32[]{:S(2)}, u32[]{:S(2)}) async-start(f32[4,1,128,1024]{3,2,1,0:T(8,128)} %y_inverse.3), calls=%async_computation.7 | async-start | bytes 4194304 | tf_op jit(solution)/shard_map/all_to_all | solution.py:427
where the time goes:
time: 347 us; the launch traced here: 342 us
  waiting for transfers between devices  152 us (44%)
  Pallas kernels  100 us (29%)
  starting transfers between devices  57.3 us (17%)
  local copies, waits for them, and re-layouts  21.5 us (6%)
  other arithmetic  11.1 us (3%)
    all_to_all x2, waiting for transfers between devices, prior(): back = [lax.all_to_all(done_y[v], 'gy', 0, 0, tiled=True) for v in turns]  42.2 us
    all_to_all x2, waiting for transfers between devices, prior(): lax.all_to_all(spec_y[v], ('gx', 'gy'), 0, 0, tiled=True)  41.4 us
    pallas_call x1, Pallas kernels, data_part(): pl.pallas_call(data_strips, grid=(1,), in_specs=[whole(q), pl.BlockSpec((...  37.5 us
    pallas_call x2, Pallas kernels, prior(): pl.pallas_call(x_apply, out_shape=packed_shape, compiler_params=params, n...  32.6 us
    all_to_all x2, waiting for transfers between devices, prior(): lax.all_to_all(done_x[v], ('gx', 'gy'), 0, 0, tiled=True)  29.8 us
    all_to_all x2, waiting for transfers between devices, prior(): lax.all_to_all(starts[v].reshape(along, 1, rows, by), 'gy', 0, 0, tiled=T...  22.4 us
    pallas_call x2, Pallas kernels, prior(): pl.pallas_call(y_inverse, out_shape=lines_shape, compiler_params=params,...  15.1 us
    pallas_call x2, Pallas kernels, prior(): pl.pallas_call(y_forward, out_shape=packed_shape, compiler_params=params,...  15 us
  transfers between devices with their start and end apart: 12, of which 11 were waited for; matrix products, arithmetic and copies ran while one was open for 6% of the time, Pallas kernels for 29%

commit v1 on v0

--- a/solution.py
+++ b/solution.py
@@ -313,63 +313,210 @@
     return [(groups[-1][0], None)] + groups[:-1] + [(groups[-1][1], None)]
 
 
-def y_forward(x_ref, hi_ref, lo_ref, out_ref):
-    parts, wide = x_ref.shape[0], x_ref.shape[-1]
-    inner = parts * wide // OUTER
+MESH = pl.DeviceIdType.MESH
+CUTS = 4
+
+
+def y_forward(lines, v, rows, mats, spec):
+    wide, width = lines.shape[-1], spec.shape[-1]
+    inner = lines.shape[1] * wide // OUTER
     per = wide // inner
-    xs = [x_ref[a // per, 0, :, (a % per) * inner : (a % per + 1) * inner] for a in range(OUTER)]
-    width = out_ref.shape[-1]
+    xs = [lines[v, a // per, rows, (a % per) * inner : (a % per + 1) * inner] for a in range(OUTER)]
     each = 2 * inner // width
     for g, (re, im) in enumerate(pairs(half_spectrum(xs))):
-        res = right(jnp.concatenate([re, im], axis=1), hi_ref[g], lo_ref[g])
+        res = right(jnp.concatenate([re, im], axis=1), mats[0, g], mats[1, g])
         for c in range(each):
-            out_ref[g * each + c, 0] = res[:, c * width : (c + 1) * width]
-
-
-def y_inverse(x_ref, hi_ref, lo_ref, out_ref):
-    parts, wide = out_ref.shape[0], out_ref.shape[-1]
-    inner = parts * wide // OUTER
+            spec[v, g * each + c, rows] = res[:, c * width : (c + 1) * width]
+
+
+def y_inverse(backs, v, rows, mats, lines):
+    wide, width = lines.shape[-1], backs.shape[-1]
+    inner = lines.shape[1] * wide // OUTER
     per = wide // inner
-    width = x_ref.shape[-1]
     each = 2 * inner // width
     groups = []
     for g in range(OUTER // 2):
-        spec = jnp.concatenate([x_ref[g * each + c, 0] for c in range(each)], axis=1)
-        res = right(spec, hi_ref[g], lo_ref[g])
+        spec = jnp.concatenate([backs[v, g * each + c, rows] for c in range(each)], axis=1)
+        res = right(spec, mats[2, g], mats[3, g])
         groups.append((res[:, :inner], res[:, inner:]))
     for a, slab in enumerate(half_spectrum_t(unpairs(groups))):
-        out_ref[a // per, 0, :, (a % per) * inner : (a % per + 1) * inner] = slab
-
-
-def x_apply(x_ref, ky_ref, kx_ref, fhi_ref, flo_ref, ihi_ref, ilo_ref, out_ref):
-    count, nvec, rows, width = x_ref.shape
+        lines[v, a // per, rows, (a % per) * inner : (a % per + 1) * inner] = slab
+
+
+def x_apply(full, v, ky, kx_ref, mats, out):
+    count, rows, width = full.shape[1:]
     inner = count * rows // OUTER
     per = inner // rows
-
-    def slab(a):
-        return jnp.concatenate(
-            [x_ref[a * per : (a + 1) * per, v].reshape(inner, width) for v in range(nvec)], axis=1
-        )
-
-    ky = jnp.concatenate([ky_ref[...]] * nvec, axis=1)
+    slabs = [full[v, a * per : (a + 1) * per].reshape(inner, width) for a in range(OUTER)]
     groups = []
-    for g, (re, im) in enumerate(pairs(half_spectrum([slab(a) for a in range(OUTER)]))):
-        spec = left(fhi_ref[g], flo_ref[g], jnp.concatenate([re, im], axis=0))
+    for g, (re, im) in enumerate(pairs(half_spectrum(slabs))):
+        spec = left(mats[2, g], mats[3, g], jnp.concatenate([re, im], axis=0))
         wave = kx_ref[g] + ky
-        res = left(ihi_ref[g], ilo_ref[g], PRIOR_GAIN * wave * wave * spec)
+        res = left(mats[0, g], mats[1, g], PRIOR_GAIN * wave * wave * spec)
         groups.append((res[:inner], res[inner:]))
     for a, res in enumerate(half_spectrum_t(unpairs(groups))):
-        for v in range(nvec):
-            out_ref[a * per : (a + 1) * per, v] = res[:, v * width : (v + 1) * width].reshape(
-                per, rows, width
-            )
+        out[v, a * per : (a + 1) * per] = res.reshape(per, rows, width)
+
+
+def settle(ref, sem):
+    pltpu.make_async_copy(ref, ref, sem).wait()
+
+
+def prior_kernel(
+    q_ref, fhi_ref, flo_ref, thi_ref, tlo_ref, ky_ref, kx_ref, out_ref,
+    lines, spec, full, backs, last, mats,
+    mat_sem, own_sem, out_sem, send_lines, get_lines, send_full, get_full,
+    send_backs, get_backs, send_last, get_last,
+):
+    across, along = lax.axis_size("gx"), lax.axis_size("gy")
+    gx, gy = lax.axis_index("gx"), lax.axis_index("gy")
+    count, me = across * along, gx * along + gy
+    nvec, bx, by = q_ref.shape
+    tall = bx // along
+    step = tall // CUTS
+    chunks = nvec * CUTS
+
+    def where(p):
+        return (lax.div(p, along), lax.rem(p, along))
+
+    def span(c):
+        return lax.div(c, CUTS), pl.multiple_of(lax.rem(c, CUTS) * step, step)
+
+    def each(total, body):
+        def run(i, carry):
+            body(i)
+            return carry
+
+        lax.fori_loop(0, total, run, 0)
+
+    barrier = pltpu.get_barrier_semaphore()
+
+    def greet(i):
+        p = lax.rem(me + 1 + i, count)
+        pl.semaphore_signal(barrier, inc=1, device_id=where(p), device_id_type=MESH)
+
+    each(count - 1, greet)
+    pl.semaphore_wait(barrier, count - 1)
+
+    def own_lines(v):
+        return pltpu.make_async_copy(
+            q_ref.at[v, pl.ds(pl.multiple_of(gy * tall, tall), tall)], lines.at[v, gy],
+            own_sem.at[v],
+        )
+
+    def start_lines(c):
+        v, first = span(c)
+
+        def one(i):
+            p = lax.rem(gy + 1 + i, along)
+            pltpu.make_async_remote_copy(
+                q_ref.at[v, pl.ds(pl.multiple_of(p * tall + first, step), step)],
+                lines.at[v, gy, pl.ds(first, step)],
+                send_lines.at[c], get_lines.at[c],
+                device_id=(gx, p), device_id_type=MESH,
+            ).start()
+
+        each(along - 1, one)
+
+    each(nvec, lambda v: own_lines(v).start())
+    each(chunks, start_lines)
+    loads = [
+        pltpu.make_async_copy(ref, mats.at[i], mat_sem.at[i])
+        for i, ref in enumerate((fhi_ref, flo_ref, thi_ref, tlo_ref))
+    ]
+    for load in loads:
+        load.start()
+    for load in loads[:2]:
+        load.wait()
+    each(nvec, lambda v: own_lines(v).wait())
+
+    def scatter(src, dst, v, first, send, get):
+        rows = pl.ds(first, step)
+        dst[v, me, rows] = src[v, me, rows]
+
+        def one(i):
+            p = lax.rem(me + 1 + i, count)
+            pltpu.make_async_remote_copy(
+                src.at[v, p, rows], dst.at[v, me, rows], send, get,
+                device_id=where(p), device_id_type=MESH,
+            ).start()
+
+        each(count - 1, one)
+
+    def forward_y(c):
+        v, first = span(c)
+        rows = pl.ds(first, step)
+        settle(lines.at[v, pl.ds(0, along - 1), rows], get_lines.at[c])
+        y_forward(lines, v, rows, mats, spec)
+        scatter(spec, full, v, first, send_full.at[v], get_full.at[v])
+
+    each(chunks, forward_y)
+    for load in loads[2:]:
+        load.wait()
+
+    def along_x(v):
+        settle(full.at[v, pl.ds(0, count - 1)], get_full.at[v])
+        settle(spec.at[v, pl.ds(0, count - 1)], send_full.at[v])
+        x_apply(full, v, ky_ref[pl.ds(me, 1)], kx_ref, mats, spec)
+
+        def part(h):
+            c = v * CUTS + h
+            first = pl.multiple_of(h * step, step)
+            scatter(spec, backs, v, first, send_backs.at[c], get_backs.at[c])
+
+        each(CUTS, part)
+
+    each(nvec, along_x)
+
+    def out_copy(c, s):
+        v, first = span(c)
+        rows = pl.ds(pl.multiple_of(s * tall + first, step), step)
+        return pltpu.make_async_copy(last.at[v, s, pl.ds(first, step)], out_ref.at[v, rows], out_sem.at[c, s])
+
+    def finish(c):
+        v, first = span(c)
+        settle(last.at[v, pl.ds(0, along - 1), pl.ds(first, step)], get_last.at[c])
+        each(along, lambda s: out_copy(c, s).start())
+
+    def backward_y(c):
+        v, first = span(c)
+        rows = pl.ds(first, step)
+        settle(backs.at[v, pl.ds(0, count - 1), rows], get_backs.at[c])
+        y_inverse(backs, v, rows, mats, lines)
+        last[v, gy, rows] = lines[v, gy, rows]
+
+        def one(i):
+            p = lax.rem(gy + 1 + i, along)
+            pltpu.make_async_remote_copy(
+                lines.at[v, p, rows], last.at[v, gy, rows], send_last.at[c], get_last.at[c],
+                device_id=(gx, p), device_id_type=MESH,
+            ).start()
+
+        each(along - 1, one)
+
+        @pl.when(c > 0)
+        def _():
+            finish(c - 1)
+
+    each(chunks, backward_y)
+    finish(chunks - 1)
+
+    def drain(c):
+        v, first = span(c)
+        rows = pl.ds(first, step)
+        settle(lines.at[v, pl.ds(0, along - 1), rows], send_lines.at[c])
+        settle(lines.at[v, pl.ds(0, along - 1), rows], send_last.at[c])
+        settle(spec.at[v, pl.ds(0, count - 1), rows], send_backs.at[c])
+        each(along, lambda s: out_copy(c, s).wait())
+
+    each(chunks, drain)
 
 
 def cost(flops, moved):
     return pl.CostEstimate(flops=int(flops), bytes_accessed=int(moved), transcendentals=0)
 
 
-def prior(q, heat, labels):
+def prior(q):
     across, along = lax.axis_size("gx"), lax.axis_size("gy")
     nvec, bx, by = q.shape
     length = by * along
@@ -379,53 +526,30 @@
     mats, wave = line_tables(length)
     fhi, flo = two_parts(mats)
     thi, tlo = two_parts(np.swapaxes(mats, 1, 2))
-    params = pltpu.CompilerParams(vmem_limit_bytes=VMEM_BYTES)
-    lines_shape = jax.ShapeDtypeStruct((along, 1, rows, by), jnp.float32)
-    packed_shape = jax.ShapeDtypeStruct((count, 1, rows, width), jnp.float32)
-    work = 6 * mats.size * bx * by // length
-    moved = 8 * bx * by + 4 * mats.size
-
-    me = lax.axis_index("gx") * along + lax.axis_index("gy")
-    ky = lax.dynamic_slice_in_dim(
-        jnp.asarray(wave.reshape(1, length), jnp.float32), me * width, width, axis=1
-    )
+    ky = jnp.asarray(wave.reshape(count, width), jnp.float32)
     kx = jnp.asarray(wave[:, :, None], jnp.float32)
-    turns = range(nvec)
-    starts = [q[v] for v in turns]
-    starts[-1], *rim = lax.optimization_barrier((starts[-1], *rim_rows(q, heat, labels)))
-    whole_y = [
-        lax.all_to_all(starts[v].reshape(along, 1, rows, by), "gy", 0, 0, tiled=True) for v in turns
-    ]
-    spec_y = [
-        pl.pallas_call(
-            y_forward, out_shape=packed_shape, compiler_params=params, name="y_forward",
-            cost_estimate=cost(work, moved),
-        )(whole_y[v], fhi, flo)
-        for v in turns
-    ]
-    side = rim_sides(q, heat, labels, *rim)
-    spec_y[-1], side = lax.optimization_barrier((spec_y[-1], side))
-    whole_x = [lax.all_to_all(spec_y[v], ("gx", "gy"), 0, 0, tiled=True) for v in turns]
-    done_x = [
-        pl.pallas_call(
-            x_apply, out_shape=packed_shape, compiler_params=params, name="x_apply",
-            cost_estimate=cost(4 * work, 2 * moved),
-        )(whole_x[v], ky, kx, thi, tlo, fhi, flo)
-        for v in turns
-    ]
-    done_x[-1], side = lax.optimization_barrier((done_x[-1], side))
-    data = data_part(q, heat, labels, *rim, side)
-    back_y = [lax.all_to_all(done_x[v], ("gx", "gy"), 0, 0, tiled=True) for v in turns]
-    back_y[0], data = lax.optimization_barrier((back_y[0], data))
-    done_y = [
-        pl.pallas_call(
-            y_inverse, out_shape=lines_shape, compiler_params=params, name="y_inverse",
-            cost_estimate=cost(work, moved),
-        )(back_y[v], thi, tlo)
-        for v in turns
-    ]
-    back = [lax.all_to_all(done_y[v], "gy", 0, 0, tiled=True) for v in turns]
-    return [back[v].reshape(bx, by) for v in turns], data
+    lines = pltpu.VMEM((nvec, along, rows, by), jnp.float32)
+    packed = pltpu.VMEM((nvec, count, rows, width), jnp.float32)
+    chunks = nvec * CUTS
+    dma = pltpu.SemaphoreType.DMA
+    anywhere, inside = pl.BlockSpec(memory_space=pl.ANY), pl.BlockSpec(memory_space=pltpu.VMEM)
+    return pl.pallas_call(
+        prior_kernel,
+        in_specs=[anywhere] * 5 + [inside] * 2,
+        out_specs=anywhere,
+        out_shape=jax.ShapeDtypeStruct(q.shape, jnp.float32),
+        scratch_shapes=[
+            lines, packed, packed, packed, lines, pltpu.VMEM((4,) + mats.shape, jnp.bfloat16),
+            dma((4,)), dma((nvec,)), dma((chunks, along)), dma((chunks,)), dma((chunks,)),
+            dma((nvec,)), dma((nvec,)), dma((chunks,)), dma((chunks,)), dma((chunks,)),
+            dma((chunks,)),
+        ],
+        compiler_params=pltpu.CompilerParams(
+            vmem_limit_bytes=VMEM_BYTES, collective_id=0, has_side_effects=True
+        ),
+        cost_estimate=cost(36 * mats.size * nvec * bx * by // length, 64 * nvec * bx * by),
+        name="prior",
+    )(q, fhi, flo, thi, tlo, ky, kx)
 
 
 RIM = 8
@@ -558,8 +682,9 @@
     square = bx * across == by * along
     if not square or rows % 16 or width % 128 or by % (by * along // OUTER) or bx % 32:
         return shards_general(q, heat, labels)
-    parts, data = prior(q, heat, labels)
-    return jnp.stack([data[v] + part for v, part in enumerate(parts)])
+    above, below = rim_rows(q, heat, labels)
+    side = rim_sides(q, heat, labels, above, below)
+    return data_part(q, heat, labels, above, below, side) + prior(q)
 
 
 def solution(mesh):

time: 347 us -> 302 us (0.87); the launches traced: 342 us -> 301 us
  Pallas kernels: 100 us -> 255 us
  waiting for transfers between devices: 152 us -> 0.01 us
  starting transfers between devices: 57.3 us -> 11.6 us
    pallas_call x6 -> x1, Pallas kernels: 62.7 us -> 217 us  [prior(): pl.pallas_call(prior_kernel, in_specs=[anywhere] * 5 + [inside] * 2, out_...]
    all_to_all x8 -> x0, waiting for transfers between devices: 136 us -> none  [the longest x2 42.2 us: prior(): back = [lax.all_to_all(done_y[v], 'gy', 0, 0, tiled=True) for v in turns]]
    all_to_all x8 -> x0, starting transfers between devices: 46.7 us -> none  [the longest x2 14.7 us: prior(): lax.all_to_all(done_x[v], ('gx', 'gy'), 0, 0, tiled=True)]
    ppermute x1, waiting for transfers between devices: 11.5 us -> 0.01 us  [rim_rows(): lax.ppermute(near(q, heat, labels, lambda f: f[..., bx - RIM:, :]), 'gx',...]
    slice x1 -> x0, local copies, waits for them, and re-layouts: 4.83 us -> none  [prior(): starts = [q[v] for v in turns]]
    ppermute x2, waiting for transfers between devices: 4.43 us -> 0.01 us  [rim_sides(): ends.append(lax.ppermute(jnp.swapaxes(line, 1, 2), 'gy', shift('gy', step)))]
  transfers between devices with their start and end apart: 12 -> 4, of which waited for: 11 -> 0; matrix products, arithmetic and copies ran while one was open for 6% -> 6% of each run, Pallas kernels for 29% -> 72%
where the time goes in v1:
time: 302 us; the launch traced here: 301 us
  Pallas kernels  255 us (84%)
  local copies, waits for them, and re-layouts  20.1 us (7%)
  other arithmetic  13.9 us (5%)
  starting transfers between devices  11.6 us (4%)
    pallas_call x1, Pallas kernels, prior(): pl.pallas_call(prior_kernel, in_specs=[anywhere] * 5 + [inside] * 2, out_...  217 us
    pallas_call x1, Pallas kernels, data_part(): pl.pallas_call(data_strips, grid=(1,), in_specs=[whole(q), pl.BlockSpec((...  37.9 us
    slice x5, local copies, waits for them, and re-layouts, rim_sides(): f[..., cols]  7.7 us
    ppermute x2, starting transfers between devices, rim_sides(): ends.append(lax.ppermute(jnp.swapaxes(line, 1, 2), 'gy', shift('gy', step)))  6.34 us
  transfers between devices with their start and end apart: 4, of which 0 were waited for; matrix products, arithmetic and copies ran while one was open for 6% of the time, Pallas kernels for 72%

profile of v1, /device:TPU:13, one launch (start us, length us, event | category | flops | bytes accessed | tf_op | source)
XLA Modules:
  0.0 301.0 jit_solution(8025772117651418618)
XLA Ops:
  0.0 0.9 fusion.4
  0.9 1.0 fusion.2
  1.9 1.0 add_convert_fusion
  2.9 0.7 pad_maximum_fusion
  3.6 3.1 %collective-permute-start = (f32[9,8,1024]{2,1,0:T(8,128)}, f32[9,8,1024]{2,1,0:T(8,128)S(1)}, u32[]{:S(2)}, u32[]{:S(2)}) collective-permute-start(f32[9,8,1024]{2,1,0:T(8,128)} %pad_maximum_fusion), channel_id=1, source_target_pairs={{0,4},{4,8},{8,12},{12,16},{16,20},{20,24},{24,28},{1,5},{5,9},{9,... | collective-permute-start | bytes 884744 | tf_op jit(solution)/shard_map/ppermute | solution.py:577
  6.8 0.8 pad_maximum_fusion.1
  7.5 2.1 collective-permute-start.1
  9.7 2.3 fusion.3
  12.0 1.9 fusion.1
  13.9 2.9 fusion
  16.8 2.1 copy.35
  18.9 0.8 add_convert_fusion.3
  19.7 0.9 copy.37
  20.7 0.8 add_convert_fusion.2
  21.5 1.2 copy.34
  22.7 1.2 copy.36
  23.9 0.3 copy.24
  24.2 0.3 copy.29
  24.6 0.0 collective-permute-done.above_ref
  24.6 0.0 copy-start.1
  24.6 0.1 fusion.5
  24.7 0.1 copy.25
  24.7 0.1 copy.30
  24.8 0.0 collective-permute-done.1.below_ref
  24.8 0.9 fusion.6
  25.7 0.1 copy.26
  25.8 0.1 copy.31
  25.8 0.1 maximum_bitcast_fusion.2
  26.0 4.2 %collective-permute-start.3 = (f32[9,8,528]{2,1,0:T(8,128)S(1)}, f32[9,8,528]{2,1,0:T(8,128)S(1)}, u32[]{:S(2)}, u32[]{:S(2)}) collective-permute-start(f32[9,8,528]{2,1,0:T(8,128)S(1)} %maximum_bitcast_fusion.2), channel_id=1, source_target_pairs={{0,1},{1,2},{2,3},{4,5},{5,6},{6,7},{8,9},{9,10},{10,11},{12,13},{... | collective-permute-start | bytes 456200 | tf_op jit(solution)/shard_map/ppermute | solution.py:592
  30.2 0.1 maximum_bitcast_fusion.1
  30.3 2.1 collective-permute-start.2
  32.4 217.3 %prior.1 = f32[2,512,1024]{2,1,0:T(8,128)} custom-call(f32[2,512,1024]{2,1,0:T(8,128)} %q_ref.3, bf16[8,512,512]{2,1,0:T(8,128)(2,1)} %constant.19.clone.fhi_ref, bf16[8,512,512]{2,1,0:T(8,128)(2,1)} %constant.20.clone.flo_ref, bf16[8,512,512]{2,1,0:T(8,128)(2,1)} %constant.21.clone.thi_ref, bf16[8,512,512]{2,1,0:T(8,128)(2,1)} %constant.22.clone.tlo_ref, ...), custom_call_target="tpu_custom_call" | custom-call | flops 19327352832 | bytes 67108864 | tf_op jit(solution)/shard_map/prior/pallas_call | solution.py:536
  249.8 0.0 copy-done.1
  249.8 0.1 pad.1.clone
  249.9 0.0 collective-permute-done.2
  249.9 1.6 copy.32
  251.5 0.0 collective-permute-done.3
  251.5 2.1 copy.33
  253.6 3.9 %maximum_bitcast_fusion.side_ref = f32[9,528,128]{2,1,0:T(8,128)} fusion(f32[9,8,528]{1,2,0:T(8,128)} %copy.33, f32[9,8,528]{1,2,0:T(8,128)S(1)} %copy.32, f32[128]{0:T(128)S(1)} %pad.1.clone), kind=kLoop, calls=%fused_computation | loop fusion | flops 1216512 | bytes 2737664 | tf_op jit(solution)/shard_map/transpose | solution.py:594
  257.5 0.0 copy-start
  257.5 37.9 %data_strips.1 = f32[2,512,1024]{2,1,0:T(8,128)} custom-call(f32[2,512,1024]{2,1,0:T(8,128)} %q_ref.3, f32[4,512,1024]{2,1,0:T(8,128)} %bitcast.15, s32[2,2,512,1024]{3,2,1,0:T(8,128)} %labels_ref.1, f32[9,8,1024]{2,1,0:T(8,128)} %copy-done.1, f32[9,8,1024]{2,1,0:T(8,128)} %collective-permute-done.1.below_ref, f32[9,528,128]{2,1,0:T(8,128)} %maximum_bitcast_fusion.side_ref), custom_call_target="tpu_custom_call" | custom-call | flops 419430400 | bytes 25165824 | tf_op jit(solution)/shard_map/data_strips/pallas_call | solution.py:662
  295.4 0.0 copy-done
  295.4 5.6 %add.19 = f32[2,512,1024]{2,1,0:T(8,128)} add(f32[2,512,1024]{2,1,0:T(8,128)} %data_strips.1, f32[2,512,1024]{2,1,0:T(8,128)S(1)} %copy-done) | non-fusion elementwise | flops 1048576 | bytes 12582912 | tf_op jit(solution)/shard_map/add | solution.py:687
  (5 shorter events, 0.0 us)
Async XLA Ops:
  3.6 20.9 %collective-permute-start = (f32[9,8,1024]{2,1,0:T(8,128)}, f32[9,8,1024]{2,1,0:T(8,128)S(1)}, u32[]{:S(2)}, u32[]{:S(2)}) collective-permute-start(f32[9,8,1024]{2,1,0:T(8,128)} %pad_maximum_fusion), channel_id=1, source_target_pairs={{0,4},{4,8},{8,12},{12,16},{16,20},{20,24},{24,28},{1,5},{5,9},{9,... | collective-permute-start | bytes 884744 | tf_op jit(solution)/shard_map/ppermute | solution.py:577
  7.5 17.3 %collective-permute-start.1 = (f32[9,8,1024]{2,1,0:T(8,128)}, f32[9,8,1024]{2,1,0:T(8,128)}, u32[]{:S(2)}, u32[]{:S(2)}) collective-permute-start(f32[9,8,1024]{2,1,0:T(8,128)} %pad_maximum_fusion.1), channel_id=1, source_target_pairs={{4,0},{8,4},{12,8},{16,12},{20,16},{24,20},{28,24},{5,1},{9,5},{13... | collective-permute-start | bytes 884744 | tf_op jit(solution)/shard_map/ppermute | solution.py:580
  24.6 225.2 %copy-start.1 = (f32[9,8,1024]{2,1,0:T(8,128)}, f32[9,8,1024]{2,1,0:T(8,128)S(1)}, u32[]{:S(2)}) copy-start(f32[9,8,1024]{2,1,0:T(8,128)S(1)} %collective-permute-done.above_ref) | copy-start | bytes 884740
  26.0 225.5 %collective-permute-start.3 = (f32[9,8,528]{2,1,0:T(8,128)S(1)}, f32[9,8,528]{2,1,0:T(8,128)S(1)}, u32[]{:S(2)}, u32[]{:S(2)}) collective-permute-start(f32[9,8,528]{2,1,0:T(8,128)S(1)} %maximum_bitcast_fusion.2), channel_id=1, source_target_pairs={{0,1},{1,2},{2,3},{4,5},{5,6},{6,7},{8,9},{9,10},{10,11},{12,13},{... | collective-permute-start | bytes 456200 | tf_op jit(solution)/shard_map/ppermute | solution.py:592
  30.3 219.5 %collective-permute-start.2 = (f32[9,8,528]{2,1,0:T(8,128)S(1)}, f32[9,8,528]{2,1,0:T(8,128)}, u32[]{:S(2)}, u32[]{:S(2)}) collective-permute-start(f32[9,8,528]{2,1,0:T(8,128)S(1)} %maximum_bitcast_fusion.1), channel_id=1, source_target_pairs={{1,0},{2,1},{3,2},{5,4},{6,5},{7,6},{9,8},{10,9},{11,10},{13,12},{... | collective-permute-start | bytes 456200 | tf_op jit(solution)/shard_map/ppermute | solution.py:592
  257.5 37.9 %copy-start = (f32[2,512,1024]{2,1,0:T(8,128)S(1)}, f32[2,512,1024]{2,1,0:T(8,128)}, u32[]{:S(2)}) copy-start(f32[2,512,1024]{2,1,0:T(8,128)} %prior.1) | copy-start | bytes 12582916

commit v2 on v1

--- a/solution.py
+++ b/solution.py
@@ -362,11 +362,12 @@
     pltpu.make_async_copy(ref, ref, sem).wait()
 
 
-def prior_kernel(
-    q_ref, fhi_ref, flo_ref, thi_ref, tlo_ref, ky_ref, kx_ref, out_ref,
-    lines, spec, full, backs, last, mats,
+def whole_kernel(
+    q_ref, heat_ref, labels_ref, fhi_ref, flo_ref, thi_ref, tlo_ref, ky_ref, kx_ref, out_ref,
+    lines, spec, full, backs, last, mats, data, ends, edges, packs, strips,
     mat_sem, own_sem, out_sem, send_lines, get_lines, send_full, get_full,
     send_backs, get_backs, send_last, get_last,
+    send_ends, get_ends, edge_sem, send_packs, get_packs, strip_sem,
 ):
     across, along = lax.axis_size("gx"), lax.axis_size("gy")
     gx, gy = lax.axis_index("gx"), lax.axis_index("gy")
@@ -419,13 +420,52 @@
         each(along - 1, one)
 
     each(nvec, lambda v: own_lines(v).start())
-    each(chunks, start_lines)
+    start_lines(0)
+    sources = (q_ref, heat_ref, labels_ref)
+
+    def end_copy(side, kind, target):
+        src, dst = sources[kind], ends[kind]
+        first = bx - RIM if side == 0 else 0
+        return pltpu.make_async_remote_copy(
+            src.at[pl.ds(0, dst.shape[1]), pl.ds(first, RIM)], dst.at[side],
+            send_ends.at[side, kind], get_ends.at[side, kind],
+            device_id=(target, gy), device_id_type=MESH,
+        )
+
+    def edge_copy(side, kind):
+        src, dst = sources[kind], edges[kind]
+        return pltpu.make_async_copy(
+            src.at[pl.ds(0, dst.shape[1]), :, pl.ds(by - 128 if side else 0, 128)], dst.at[side],
+            edge_sem.at[side, kind],
+        )
+
+    for side, (sends, target) in enumerate(((gx < across - 1, gx + 1), (gx > 0, gx - 1))):
+
+        @pl.when(sends)
+        def _():
+            for kind in range(3):
+                end_copy(side, kind, target).start()
+
+        @pl.when(gx == (0 if side == 0 else across - 1))
+        def _():
+            for kind in range(3):
+                ref = ends[kind]
+                ref[side] = jnp.full(ref.shape[1:], -1 if kind == 2 else 0, ref.dtype)
+
+        @pl.when(gy == (along - 1 if side == 0 else 0))
+        def _():
+            packs[2 + side] = jnp.zeros(packs.shape[1:], jnp.float32)
+
     loads = [
         pltpu.make_async_copy(ref, mats.at[i], mat_sem.at[i])
         for i, ref in enumerate((fhi_ref, flo_ref, thi_ref, tlo_ref))
     ]
     for load in loads:
         load.start()
+    each(chunks - 1, lambda c: start_lines(c + 1))
+    for side in range(2):
+        for kind in range(3):
+            edge_copy(side, kind).start()
     for load in loads[:2]:
         load.wait()
     each(nvec, lambda v: own_lines(v).wait())
@@ -450,11 +490,125 @@
         y_forward(lines, v, rows, mats, spec)
         scatter(spec, full, v, first, send_full.at[v], get_full.at[v])
 
-    each(chunks, forward_y)
+    each(CUTS, forward_y)
+
+    def packed(side, fields):
+        lane = lax.broadcasted_iota(jnp.int32, fields[0].shape, 1)
+        total = jnp.zeros(fields[0].shape, jnp.float32)
+        for i, f in enumerate(fields):
+            moved = pltpu.roll(f, RIM * (i + side), 1)
+            total = jnp.where((lane >= RIM * i) & (lane < RIM * (i + 1)), moved, total)
+        return total
+
+    def nine(q, level, label):
+        return (
+            [q(v) for v in range(nvec)]
+            + [(label(i) + 1).astype(jnp.float32) for i in range(4)]
+            + [level(i) for i in range(3)]
+        )
+
+    for side, gets in enumerate((gx > 0, gx < across - 1)):
+
+        @pl.when(gets)
+        def _():
+            for kind in range(3):
+                settle(ends[kind].at[side], get_ends.at[side, kind])
+
+    for side in range(2):
+        for kind in range(3):
+            edge_copy(side, kind).wait()
+        cols = slice(by - 128, by) if side else slice(0, 128)
+        for end, at in ((0, 0), (1, RIM + bx)):
+            packs[side, at : at + RIM] = packed(
+                side, nine(*[lambda i, r=r: r[end, i, :, cols] for r in ends])
+            )
+
+        def pack_some(n):
+            first = pl.multiple_of(n * 64, 64)
+            packs[side, pl.ds(pl.multiple_of(first + RIM, RIM), 64)] = packed(
+                side, nine(*[lambda i, r=r: r[side, i, pl.ds(first, 64)] for r in edges])
+            )
+
+        each(bx // 64, pack_some)
+
+    def pack_copy(side, target):
+        return pltpu.make_async_remote_copy(
+            packs.at[side], packs.at[2 + side], send_packs.at[side], get_packs.at[side],
+            device_id=(gx, target), device_id_type=MESH,
+        )
+
+    for side, (sends, target) in enumerate(((gy > 0, gy - 1), (gy < along - 1, gy + 1))):
+
+        @pl.when(sends)
+        def _():
+            pack_copy(side, target).start()
+
+    total = bx // STRIP
+    strip_tall = STRIP + 2 * RIM
+
+    def strip_copy(s, slot):
+        for kind in range(3):
+            src, dst, sem = sources[kind], strips[kind], strip_sem.at[slot, kind]
+            depth = pl.ds(0, dst.shape[1])
+
+            @pl.when((s > 0) & (s < total - 1))
+            def _():
+                rows = pl.ds(pl.multiple_of(s * STRIP - RIM, RIM), strip_tall)
+                pltpu.make_async_copy(src.at[depth, rows], dst.at[slot], sem).start()
+
+            for edge, side, near_at, far_at, from_at in (
+                (0, 0, 0, RIM, 0),
+                (total - 1, 1, STRIP + RIM, 0, bx - STRIP - RIM),
+            ):
+
+                @pl.when(s == edge)
+                def _():
+                    pltpu.make_async_copy(
+                        ends[kind].at[side], dst.at[slot, :, pl.ds(near_at, RIM)], sem
+                    ).start()
+                    pltpu.make_async_copy(
+                        src.at[depth, pl.ds(from_at, STRIP + RIM)],
+                        dst.at[slot, :, pl.ds(far_at, STRIP + RIM)],
+                        sem,
+                    ).start()
+
+    def strip_work(s):
+        slot = lax.rem(s, 2)
+        for kind in range(3):
+            settle(strips[kind].at[slot], strip_sem.at[slot, kind])
+
+        @pl.when(s + 1 < total)
+        def _():
+            strip_copy(s + 1, 1 - slot)
+
+        first = pl.multiple_of(s * STRIP, STRIP)
+        over, under = (packs[side, pl.ds(first, strip_tall)] for side in (2, 3))
+        lane = lax.broadcasted_iota(jnp.int32, over.shape, 1)
+
+        def side_of(i):
+            return jnp.where(
+                lane < RIM,
+                pltpu.roll(over, (128 - RIM * i) % 128, 1),
+                jnp.where(lane >= 128 - RIM, pltpu.roll(under, 128 - RIM - RIM * i, 1), 0.0),
+            )
+
+        middle = nine(*[lambda i, r=r: r[slot, i] for r in strips])
+        fields = [jnp.concatenate([f, side_of(i)], axis=1) for i, f in enumerate(middle)]
+        for v, res in enumerate(data_strip(fields, nvec)):
+            data[v, pl.ds(first, STRIP)] = res[RIM : RIM + STRIP, :by]
+
+    strip_copy(jnp.int32(0), 0)
+    each(chunks - CUTS, lambda c: forward_y(c + CUTS))
     for load in loads[2:]:
         load.wait()
+    for side, gets in enumerate((gy < along - 1, gy > 0)):
+
+        @pl.when(gets)
+        def _():
+            settle(packs.at[2 + side], get_packs.at[side])
 
     def along_x(v):
+        each(total // nvec, lambda i: strip_work(v * (total // nvec) + i))
         settle(full.at[v, pl.ds(0, count - 1)], get_full.at[v])
         settle(spec.at[v, pl.ds(0, count - 1)], send_full.at[v])
         x_apply(full, v, ky_ref[pl.ds(me, 1)], kx_ref, mats, spec)
@@ -471,12 +625,18 @@
     def out_copy(c, s):
         v, first = span(c)
         rows = pl.ds(pl.multiple_of(s * tall + first, step), step)
-        return pltpu.make_async_copy(last.at[v, s, pl.ds(first, step)], out_ref.at[v, rows], out_sem.at[c, s])
+        return pltpu.make_async_copy(data.at[v, rows], out_ref.at[v, rows], out_sem.at[c, s])
 
     def finish(c):
         v, first = span(c)
         settle(last.at[v, pl.ds(0, along - 1), pl.ds(first, step)], get_last.at[c])
-        each(along, lambda s: out_copy(c, s).start())
+
+        def one(s):
+            rows = pl.ds(pl.multiple_of(s * tall + first, step), step)
+            data[v, rows] = data[v, rows] + last[v, s, pl.ds(first, step)]
+            out_copy(c, s).start()
+
+        each(along, one)
 
     def backward_y(c):
         v, first = span(c)
@@ -510,13 +670,25 @@
         each(along, lambda s: out_copy(c, s).wait())
 
     each(chunks, drain)
+    for side, sends in enumerate((gx < across - 1, gx > 0)):
+
+        @pl.when(sends)
+        def _():
+            for kind in range(3):
+                settle(ends[kind].at[side], send_ends.at[side, kind])
+
+    for side, sends in enumerate((gy > 0, gy < along - 1)):
+
+        @pl.when(sends)
+        def _():
+            settle(packs.at[side], send_packs.at[side])
 
 
 def cost(flops, moved):
     return pl.CostEstimate(flops=int(flops), bytes_accessed=int(moved), transcendentals=0)
 
 
-def prior(q):
+def whole(q, heat, labels):
     across, along = lax.axis_size("gx"), lax.axis_size("gy")
     nvec, bx, by = q.shape
     length = by * along
@@ -531,148 +703,81 @@
     lines = pltpu.VMEM((nvec, along, rows, by), jnp.float32)
     packed = pltpu.VMEM((nvec, count, rows, width), jnp.float32)
     chunks = nvec * CUTS
+    levels, labels = heat.reshape(-1, bx, by), labels.reshape(-1, bx, by)
+
+    def trio(tall, wide):
+        kinds = ((nvec, jnp.float32), (3, jnp.float32), (4, jnp.int32))
+        return tuple(pltpu.VMEM((2, depth, tall, wide), kind) for depth, kind in kinds)
+
     dma = pltpu.SemaphoreType.DMA
     anywhere, inside = pl.BlockSpec(memory_space=pl.ANY), pl.BlockSpec(memory_space=pltpu.VMEM)
     return pl.pallas_call(
-        prior_kernel,
-        in_specs=[anywhere] * 5 + [inside] * 2,
+        whole_kernel,
+        in_specs=[anywhere] * 7 + [inside] * 2,
         out_specs=anywhere,
         out_shape=jax.ShapeDtypeStruct(q.shape, jnp.float32),
         scratch_shapes=[
             lines, packed, packed, packed, lines, pltpu.VMEM((4,) + mats.shape, jnp.bfloat16),
+            pltpu.VMEM(q.shape, jnp.float32), trio(RIM, by), trio(bx, 128),
+            pltpu.VMEM((4, bx + 2 * RIM, 128), jnp.float32),
+            trio(STRIP + 2 * RIM, by),
             dma((4,)), dma((nvec,)), dma((chunks, along)), dma((chunks,)), dma((chunks,)),
             dma((nvec,)), dma((nvec,)), dma((chunks,)), dma((chunks,)), dma((chunks,)),
-            dma((chunks,)),
+            dma((chunks,)), dma((2, 3)), dma((2, 3)), dma((2, 3)), dma((2,)), dma((2,)), dma((2, 3)),
         ],
         compiler_params=pltpu.CompilerParams(
             vmem_limit_bytes=VMEM_BYTES, collective_id=0, has_side_effects=True
         ),
         cost_estimate=cost(36 * mats.size * nvec * bx * by // length, 64 * nvec * bx * by),
-        name="prior",
-    )(q, fhi, flo, thi, tlo, ky, kx)
+        name="whole",
+    )(q, levels, labels, fhi, flo, thi, tlo, ky, kx)
 
 
 RIM = 8
-VMEM_BYTES = 58 * 2**20
-
-
-def shift(axis, step):
-    count = lax.axis_size(axis)
-    return [(i, i + step) for i in range(count) if 0 <= i + step < count]
-
-
-def near(q, heat, labels, cut):
-    first = cut(q)
-    return jnp.concatenate(
-        [
-            first,
-            (cut(labels) + 1).astype(jnp.float32).reshape((-1,) + first.shape[1:]),
-            cut(heat).reshape((-1,) + first.shape[1:])[:-1],
-        ]
-    )
-
-
-def rim_rows(q, heat, labels):
-    bx = q.shape[1]
-    above = lax.ppermute(
-        near(q, heat, labels, lambda f: f[..., bx - RIM :, :]), "gx", shift("gx", 1)
-    )
-    below = lax.ppermute(near(q, heat, labels, lambda f: f[..., :RIM, :]), "gx", shift("gx", -1))
-    return above, below
-
-
-def rim_sides(q, heat, labels, above, below):
-    by = q.shape[2]
-    ends = []
-    for cols, step in ((slice(0, RIM), -1), (slice(by - RIM, by), 1)):
-        line = jnp.concatenate(
-            [above[..., cols], near(q, heat, labels, lambda f: f[..., cols]), below[..., cols]],
-            axis=1,
-        )
-        ends.append(lax.ppermute(jnp.swapaxes(line, 1, 2), "gy", shift("gy", step)))
-    gap = jnp.zeros((ends[0].shape[0], 128 - 2 * RIM, ends[0].shape[2]), jnp.float32)
-    return jnp.swapaxes(jnp.concatenate([ends[0], gap, ends[1]], axis=1), 1, 2)
-
-
-def data_strips(q_ref, heat_ref, labels_ref, above_ref, below_ref, side_ref, out_ref, f_ref):
-    nvec, bx, by = out_ref.shape
-    f_ref[:, :RIM, :by] = above_ref[...]
-    f_ref[:, RIM + bx :, :by] = below_ref[...]
-    f_ref[:, :, by:] = side_ref[...]
-    levels_at = nvec + 4
-    for v in range(nvec):
-        f_ref[v, RIM : RIM + bx, :by] = q_ref[v]
-    for i in range(4):
-        f_ref[nvec + i, RIM : RIM + bx, :by] = (labels_ref[i // 2, i % 2] + 1).astype(jnp.float32)
-    for i in range(3):
-        f_ref[levels_at + i, RIM : RIM + bx, :by] = heat_ref[i]
-    strip = 32
-    tall, wide = strip + 2 * RIM, f_ref.shape[2]
+VMEM_BYTES = 60 * 2**20
+
+
+STRIP = 32
+
+
+def data_strip(fields, nvec):
+    tall, wide = fields[0].shape
 
     def rim(f):
         return (pltpu.roll(f, 1, 0) + pltpu.roll(f, tall - 1, 0)) + (
             pltpu.roll(f, 1, 1) + pltpu.roll(f, wide - 1, 1)
         )
 
-    def one(s, carry):
-        first = pl.multiple_of(s * strip, strip)
-        field = lambda i: f_ref[i, pl.ds(first, tall), :]
-
-        def inverse_capacity(label):
-            return jnp.where(label == 2.0, 0.25, jnp.where(label == 3.0, 0.8, 1.0))
-
-        def conduct(label, level):
-            base = jnp.where(
-                label == 1.0, 1.0, jnp.where(label == 2.0, 0.6, jnp.where(label == 3.0, 0.35, 0.0))
-            )
-            return TIME_STEP * base * (1.0 + 0.5 * jnp.tanh(level))
-
-        label = [field(nvec + i) for i in range(4)]
-        ic_top0, ic_top1 = inverse_capacity(label[0]), inverse_capacity(label[2])
-        ic_low1 = inverse_capacity(label[3])
-        c_top0 = conduct(label[0], field(nvec + 4))
-        c_low0 = conduct(label[1], field(nvec + 5))
-        c_top1 = conduct(label[2], field(nvec + 6))
-        for v in range(nvec):
-            q = field(v)
-            first_u = TIME_STEP * q * ic_top0
-            second_top = (2.0 * TIME_STEP) * q + c_top0 * (rim(first_u) - 6.0 * first_u)
-            top_u = second_top * ic_top1
-            low_u = c_low0 * first_u * ic_low1
-            third_top = (
-                second_top + c_top1 * (rim(top_u) - 6.0 * top_u + low_u) + TIME_STEP * q
-            )
-            adj_three = OBS_WEIGHT * third_top * ic_top1 * ic_top1
-            push_top = c_top1 * adj_three
-            adj_two = adj_three + (rim(push_top) - 6.0 * push_top) * ic_top1
-            pull_top = c_top0 * adj_two
-            pull_low = c_low0 * (push_top * ic_low1)
-            adj_one = adj_two + (rim(pull_top) - 6.0 * pull_top + pull_low) * ic_top0
-            total = TIME_STEP * (adj_three + adj_two + adj_one)
-            out_ref[v, pl.ds(first, strip), :] = total[RIM : RIM + strip, :by]
-        return carry
-
-    lax.fori_loop(0, bx // strip, one, 0)
-
-
-def data_part(q, heat, labels, above, below, side):
-    nvec, bx, by = q.shape
-    levels = heat.reshape(-1, bx, by)
-    whole = lambda x: pl.BlockSpec(x.shape, lambda i: (0,) * x.ndim)
-    return pl.pallas_call(
-        data_strips,
-        grid=(1,),
-        in_specs=[
-            whole(q), pl.BlockSpec((3, bx, by), lambda i: (0, 0, 0)), whole(labels),
-            whole(above), whole(below), whole(side),
-        ],
-        out_specs=whole(q),
-        out_shape=jax.ShapeDtypeStruct(q.shape, jnp.float32),
-        scratch_shapes=[pltpu.VMEM((nvec + 7, bx + 2 * RIM, by + 128), jnp.float32)],
-        compiler_params=pltpu.CompilerParams(vmem_limit_bytes=VMEM_BYTES),
-        cost_estimate=cost(400 * q.size, 24 * q.size),
-        name="data_strips",
-    )(q, levels, labels, above, below, side)
+    def inverse_capacity(label):
+        return jnp.where(label == 2.0, 0.25, jnp.where(label == 3.0, 0.8, 1.0))
+
+    def conduct(label, level):
+        base = jnp.where(
+            label == 1.0, 1.0, jnp.where(label == 2.0, 0.6, jnp.where(label == 3.0, 0.35, 0.0))
+        )
+        return TIME_STEP * base * (1.0 + 0.5 * jnp.tanh(level))
+
+    label = fields[nvec : nvec + 4]
+    level = fields[nvec + 4 :]
+    ic_top0, ic_top1 = inverse_capacity(label[0]), inverse_capacity(label[2])
+    ic_low1 = inverse_capacity(label[3])
+    c_top0, c_low0 = conduct(label[0], level[0]), conduct(label[1], level[1])
+    c_top1 = conduct(label[2], level[2])
+    out = []
+    for q in fields[:nvec]:
+        first_u = TIME_STEP * q * ic_top0
+        second_top = (2.0 * TIME_STEP) * q + c_top0 * (rim(first_u) - 6.0 * first_u)
+        top_u = second_top * ic_top1
+        low_u = c_low0 * first_u * ic_low1
+        third_top = second_top + c_top1 * (rim(top_u) - 6.0 * top_u + low_u) + TIME_STEP * q
+        adj_three = OBS_WEIGHT * third_top * ic_top1 * ic_top1
+        push_top = c_top1 * adj_three
+        adj_two = adj_three + (rim(push_top) - 6.0 * push_top) * ic_top1
+        pull_top = c_top0 * adj_two
+        pull_low = c_low0 * (push_top * ic_low1)
+        adj_one = adj_two + (rim(pull_top) - 6.0 * pull_top + pull_low) * ic_top0
+        out.append(TIME_STEP * (adj_three + adj_two + adj_one))
+    return out
 
 
 def shards(q, heat, labels):
@@ -680,11 +785,9 @@
     along, across = lax.axis_size("gy"), lax.axis_size("gx")
     rows, width = bx // along, by // across
     square = bx * across == by * along
-    if not square or rows % 16 or width % 128 or by % (by * along // OUTER) or bx % 32:
+    if not square or rows % 16 or width % 128 or by % (by * along // OUTER) or bx % (STRIP * nvec):
         return shards_general(q, heat, labels)
-    above, below = rim_rows(q, heat, labels)
-    side = rim_sides(q, heat, labels, above, below)
-    return data_part(q, heat, labels, above, below, side) + prior(q)
+    return whole(q, heat, labels)
 
 
 def solution(mesh):

time: 302 us -> 221 us (0.73)
  Pallas kernels: 255 us -> 214 us
  local copies, waits for them, and re-layouts: 20.1 us -> 4.79 us
  other arithmetic: 13.9 us -> 0 us
  starting transfers between devices: 11.6 us -> 0 us
    pallas_call x2 -> x1, Pallas kernels: 255 us -> 214 us  [whole(): pl.pallas_call(whole_kernel, in_specs=[anywhere] * 7 + [inside] * 2, out_...]
    ppermute x4 -> x0, starting transfers between devices: 11.6 us -> none  [the longest x2 6.34 us: rim_sides(): ends.append(lax.ppermute(jnp.swapaxes(line, 1, 2), 'gy', shift('gy', step)))]
    slice x17 -> x0, local copies, waits for them, and re-layouts: 10.8 us -> none  [the longest x5 7.7 us: rim_sides(): f[..., cols]]
    add x1 -> x0, other arithmetic: 5.57 us -> none  [shards(): return data_part(q, heat, labels, above, below, side) + prior(q)]
    transpose x3 -> x0, other arithmetic: 4.12 us -> none  [the longest x1 3.86 us: rim_sides(): return jnp.swapaxes(jnp.concatenate([ends[0], gap, ends[1]], axis=1), 1, 2)]
    ppermute x2 -> x0, local copies, waits for them, and re-layouts: 3.75 us -> none  [rim_sides(): ends.append(lax.ppermute(jnp.swapaxes(line, 1, 2), 'gy', shift('gy', step)))]
  transfers between devices with their start and end apart: 4 -> 0, of which waited for: 0 -> 0; matrix products, arithmetic and copies ran while one was open for 6% -> 0% of each run, Pallas kernels for 72% -> 0%
where the time goes in v2:
time: 221 us; the launch traced here: 219 us
  Pallas kernels  214 us (97%)
  local copies, waits for them, and re-layouts  4.79 us (2%)
    pallas_call x1, Pallas kernels, whole(): pl.pallas_call(whole_kernel, in_specs=[anywhere] * 7 + [inside] * 2, out_...  214 us
    unnamed x1, local copies, waits for them, and re-layouts  4.79 us

profile of v2, /device:TPU:13, one launch (start us, length us, event | category | flops | bytes accessed | tf_op | source)
XLA Modules:
  0.0 218.9 jit_solution(13187296379982985972)
XLA Ops:
  0.0 214.1 %whole.1 = f32[2,512,1024]{2,1,0:T(8,128)} custom-call(f32[2,512,1024]{2,1,0:T(8,128)} %q_ref.1, f32[4,512,1024]{2,1,0:T(8,128)} %bitcast.2, s32[4,512,1024]{2,1,0:T(8,128)} %bitcast.3, bf16[8,512,512]{2,1,0:T(8,128)(2,1)} %constant.14.clone.fhi_ref, bf16[8,512,512]{2,1,0:T(8,128)(2,1)} %constant.15.clone.flo_ref, ...), custom_call_target="tpu_custom_call" | custom-call | flops 19327352832 | bytes 67108864 | tf_op jit(solution)/shard_map/whole/pallas_call | solution.py:714
  214.1 4.8 %copy.11 = f32[2,512,1024]{2,1,0:T(8,128)} copy(f32[2,512,1024]{2,1,0:T(8,128)} %whole.1) | data formatting | bytes 8388608

commit v3 on v2

--- a/solution.py
+++ b/solution.py
@@ -296,12 +296,14 @@
 
 def right(x, hi, lo):
     top, rest = split(x)
-    return dot32(top, hi) + (dot32(rest, hi) + dot32(top, lo))
+    both = dot32(jnp.concatenate([top, rest], axis=0), hi)
+    return both[: x.shape[0]] + (both[x.shape[0] :] + dot32(top, lo))
 
 
 def left(hi, lo, x):
     top, rest = split(x)
-    return dot32(hi, top) + (dot32(lo, top) + dot32(hi, rest))
+    both = dot32(hi, jnp.concatenate([top, rest], axis=1))
+    return both[:, : x.shape[1]] + (dot32(lo, top) + both[:, x.shape[1] :])
 
 
 def pairs(spec):
@@ -314,7 +316,14 @@
 
 
 MESH = pl.DeviceIdType.MESH
-CUTS = 4
+CUTS = 8
+LEAD = 16
+PACK_AT = 3
+STRIPS_AT = 16
+X_AT = 18
+X_STEP = 14
+BACK_AT = 28
+LAG = 4
 
 
 def y_forward(lines, v, rows, mats, spec):
@@ -343,7 +352,19 @@
         lines[v, a // per, rows, (a % per) * inner : (a % per + 1) * inner] = slab
 
 
-def x_apply(full, v, ky, kx_ref, mats, out):
+def wave_of(g, inner, width, length):
+    row = lax.broadcasted_iota(jnp.int32, (2 * inner, width), 0)
+    place = row % inner
+    if g < OUTER // 2 - 1:
+        k = g + 1 + OUTER * place
+    else:
+        k = jnp.where(row < inner, 0, OUTER // 2) + OUTER * (place % (inner // 2))
+        k = jnp.where(row == inner // 2, length // 2, k)
+    k = jnp.where(k < length // 2, k, k - length).astype(jnp.float32) * (2.0 * math.pi / length)
+    return k * k
+
+
+def x_apply(full, v, ky, mats, out):
     count, rows, width = full.shape[1:]
     inner = count * rows // OUTER
     per = inner // rows
@@ -351,7 +372,7 @@
     groups = []
     for g, (re, im) in enumerate(pairs(half_spectrum(slabs))):
         spec = left(mats[2, g], mats[3, g], jnp.concatenate([re, im], axis=0))
-        wave = kx_ref[g] + ky
+        wave = wave_of(g, inner, width, count * rows) + ky
         res = left(mats[0, g], mats[1, g], PRIOR_GAIN * wave * wave * spec)
         groups.append((res[:inner], res[inner:]))
     for a, res in enumerate(half_spectrum_t(unpairs(groups))):
@@ -363,9 +384,9 @@
 
 
 def whole_kernel(
-    q_ref, heat_ref, labels_ref, fhi_ref, flo_ref, thi_ref, tlo_ref, ky_ref, kx_ref, out_ref,
-    lines, spec, full, backs, last, mats, data, ends, edges, packs, strips,
-    mat_sem, own_sem, out_sem, send_lines, get_lines, send_full, get_full,
+    q_ref, heat_ref, labels_ref, fhi_ref, flo_ref, thi_ref, tlo_ref, ky_ref, data,
+    lines, spec, full, backs, last, mats, ends, edges, packs, strips,
+    mat_sem, own_sem, send_lines, get_lines, send_full, get_full,
     send_backs, get_backs, send_last, get_last,
     send_ends, get_ends, edge_sem, send_packs, get_packs, strip_sem,
 ):
@@ -390,20 +411,27 @@
 
         lax.fori_loop(0, total, run, 0)
 
-    barrier = pltpu.get_barrier_semaphore()
-
-    def greet(i):
-        p = lax.rem(me + 1 + i, count)
-        pl.semaphore_signal(barrier, inc=1, device_id=where(p), device_id_type=MESH)
-
-    each(count - 1, greet)
-    pl.semaphore_wait(barrier, count - 1)
-
     def own_lines(v):
         return pltpu.make_async_copy(
             q_ref.at[v, pl.ds(pl.multiple_of(gy * tall, tall), tall)], lines.at[v, gy],
             own_sem.at[v],
         )
+
+    loads = [
+        pltpu.make_async_copy(ref, mats.at[i], mat_sem.at[i])
+        for i, ref in enumerate((fhi_ref, flo_ref, thi_ref, tlo_ref))
+    ]
+    each(nvec, lambda v: own_lines(v).start())
+    for load in loads[:2]:
+        load.start()
+    barrier = pltpu.get_barrier_semaphore()
+
+    def greet(i):
+        p = lax.rem(me + 1 + i, count)
+        pl.semaphore_signal(barrier, inc=1, device_id=where(p), device_id_type=MESH)
+
+    each(count - 1, greet)
+    pl.semaphore_wait(barrier, count - 1)
 
     def start_lines(c):
         v, first = span(c)
@@ -419,7 +447,6 @@
 
         each(along - 1, one)
 
-    each(nvec, lambda v: own_lines(v).start())
     start_lines(0)
     sources = (q_ref, heat_ref, labels_ref)
 
@@ -435,7 +462,7 @@
     def edge_copy(side, kind):
         src, dst = sources[kind], edges[kind]
         return pltpu.make_async_copy(
-            src.at[pl.ds(0, dst.shape[1]), :, pl.ds(by - 128 if side else 0, 128)], dst.at[side],
+            src.at[pl.ds(0, dst.shape[0]), :, pl.ds(by - 128 if side else 0, 128)], dst,
             edge_sem.at[side, kind],
         )
 
@@ -456,19 +483,14 @@
         def _():
             packs[2 + side] = jnp.zeros(packs.shape[1:], jnp.float32)
 
-    loads = [
-        pltpu.make_async_copy(ref, mats.at[i], mat_sem.at[i])
-        for i, ref in enumerate((fhi_ref, flo_ref, thi_ref, tlo_ref))
-    ]
-    for load in loads:
-        load.start()
-    each(chunks - 1, lambda c: start_lines(c + 1))
-    for side in range(2):
-        for kind in range(3):
-            edge_copy(side, kind).start()
+    each(LEAD - 1, lambda c: start_lines(c + 1))
     for load in loads[:2]:
         load.wait()
     each(nvec, lambda v: own_lines(v).wait())
+    for kind in range(3):
+        edge_copy(0, kind).start()
+    for load in loads[2:]:
+        load.start()
 
     def scatter(src, dst, v, first, send, get):
         rows = pl.ds(first, step)
@@ -487,10 +509,13 @@
         v, first = span(c)
         rows = pl.ds(first, step)
         settle(lines.at[v, pl.ds(0, along - 1), rows], get_lines.at[c])
+
+        @pl.when(c + LEAD < chunks)
+        def _():
+            start_lines(c + LEAD)
+
         y_forward(lines, v, rows, mats, spec)
         scatter(spec, full, v, first, send_full.at[v], get_full.at[v])
-
-    each(CUTS, forward_y)
 
     def packed(side, fields):
         lane = lax.broadcasted_iota(jnp.int32, fields[0].shape, 1)
@@ -507,41 +532,11 @@
             + [level(i) for i in range(3)]
         )
 
-    for side, gets in enumerate((gx > 0, gx < across - 1)):
-
-        @pl.when(gets)
-        def _():
-            for kind in range(3):
-                settle(ends[kind].at[side], get_ends.at[side, kind])
-
-    for side in range(2):
-        for kind in range(3):
-            edge_copy(side, kind).wait()
-        cols = slice(by - 128, by) if side else slice(0, 128)
-        for end, at in ((0, 0), (1, RIM + bx)):
-            packs[side, at : at + RIM] = packed(
-                side, nine(*[lambda i, r=r: r[end, i, :, cols] for r in ends])
-            )
-
-        def pack_some(n):
-            first = pl.multiple_of(n * 64, 64)
-            packs[side, pl.ds(pl.multiple_of(first + RIM, RIM), 64)] = packed(
-                side, nine(*[lambda i, r=r: r[side, i, pl.ds(first, 64)] for r in edges])
-            )
-
-        each(bx // 64, pack_some)
-
     def pack_copy(side, target):
         return pltpu.make_async_remote_copy(
             packs.at[side], packs.at[2 + side], send_packs.at[side], get_packs.at[side],
             device_id=(gx, target), device_id_type=MESH,
         )
-
-    for side, (sends, target) in enumerate(((gy > 0, gy - 1), (gy < along - 1, gy + 1))):
-
-        @pl.when(sends)
-        def _():
-            pack_copy(side, target).start()
 
     total = bx // STRIP
     strip_tall = STRIP + 2 * RIM
@@ -597,21 +592,56 @@
         for v, res in enumerate(data_strip(fields, nvec)):
             data[v, pl.ds(first, STRIP)] = res[RIM : RIM + STRIP, :by]
 
-    strip_copy(jnp.int32(0), 0)
-    each(chunks - CUTS, lambda c: forward_y(c + CUTS))
-    for load in loads[2:]:
-        load.wait()
-    for side, gets in enumerate((gy < along - 1, gy > 0)):
-
-        @pl.when(gets)
+    def pack_edges():
+        for side, gets in enumerate((gx > 0, gx < across - 1)):
+
+            @pl.when(gets)
+            def _():
+                for kind in range(3):
+                    settle(ends[kind].at[side], get_ends.at[side, kind])
+
+        for side in range(2):
+            for kind in range(3):
+                edge_copy(side, kind).wait()
+            cols = slice(by - 128, by) if side else slice(0, 128)
+            for end, at in ((0, 0), (1, RIM + bx)):
+                packs[side, at : at + RIM] = packed(
+                    side, nine(*[lambda i, r=r: r[end, i, :, cols] for r in ends])
+                )
+
+            def pack_some(n):
+                first = pl.multiple_of(n * 64, 64)
+                packs[side, pl.ds(pl.multiple_of(first + RIM, RIM), 64)] = packed(
+                    side, nine(*[lambda i, r=r: r[i, pl.ds(first, 64)] for r in edges])
+                )
+
+            each(bx // 64, pack_some)
+            for kind in range(3 if side == 0 else 0):
+                edge_copy(1, kind).start()
+
+        for side, (sends, target) in enumerate(((gy > 0, gy - 1), (gy < along - 1, gy + 1))):
+
+            @pl.when(sends)
+            def _():
+                pack_copy(side, target).start()
+        strip_copy(jnp.int32(0), 0)
+
+    def get_edges():
+        for side, gets in enumerate((gy < along - 1, gy > 0)):
+
+            @pl.when(gets)
+            def _():
+                settle(packs.at[2 + side], get_packs.at[side])
+
+    def along_x(v):
+        @pl.when(v == 0)
         def _():
-            settle(packs.at[2 + side], get_packs.at[side])
-
-    def along_x(v):
-        each(total // nvec, lambda i: strip_work(v * (total // nvec) + i))
+            for load in loads[2:]:
+                load.wait()
+
         settle(full.at[v, pl.ds(0, count - 1)], get_full.at[v])
         settle(spec.at[v, pl.ds(0, count - 1)], send_full.at[v])
-        x_apply(full, v, ky_ref[pl.ds(me, 1)], kx_ref, mats, spec)
+        x_apply(full, v, ky_ref[pl.ds(me, 1)], mats, spec)
 
         def part(h):
             c = v * CUTS + h
@@ -620,13 +650,6 @@
 
         each(CUTS, part)
 
-    each(nvec, along_x)
-
-    def out_copy(c, s):
-        v, first = span(c)
-        rows = pl.ds(pl.multiple_of(s * tall + first, step), step)
-        return pltpu.make_async_copy(data.at[v, rows], out_ref.at[v, rows], out_sem.at[c, s])
-
     def finish(c):
         v, first = span(c)
         settle(last.at[v, pl.ds(0, along - 1), pl.ds(first, step)], get_last.at[c])
@@ -634,7 +657,6 @@
         def one(s):
             rows = pl.ds(pl.multiple_of(s * tall + first, step), step)
             data[v, rows] = data[v, rows] + last[v, s, pl.ds(first, step)]
-            out_copy(c, s).start()
 
         each(along, one)
 
@@ -654,12 +676,18 @@
 
         each(along - 1, one)
 
-        @pl.when(c > 0)
-        def _():
-            finish(c - 1)
-
-    each(chunks, backward_y)
-    finish(chunks - 1)
+    def tick(t):
+        pl.when(t < chunks)(lambda: forward_y(t))
+        pl.when(t == PACK_AT)(pack_edges)
+        pl.when(t == STRIPS_AT)(get_edges)
+        pl.when((t >= STRIPS_AT) & (t < STRIPS_AT + total))(lambda: strip_work(t - STRIPS_AT))
+        pl.when((t >= X_AT) & (t < X_AT + X_STEP * nvec) & (lax.rem(t - X_AT, X_STEP) == 0))(
+            lambda: along_x(lax.div(t - X_AT, X_STEP))
+        )
+        pl.when((t >= BACK_AT) & (t < BACK_AT + chunks))(lambda: backward_y(t - BACK_AT))
+        pl.when(t >= BACK_AT + LAG)(lambda: finish(t - BACK_AT - LAG))
+
+    each(BACK_AT + chunks + LAG, tick)
 
     def drain(c):
         v, first = span(c)
@@ -667,7 +695,6 @@
         settle(lines.at[v, pl.ds(0, along - 1), rows], send_lines.at[c])
         settle(lines.at[v, pl.ds(0, along - 1), rows], send_last.at[c])
         settle(spec.at[v, pl.ds(0, count - 1), rows], send_backs.at[c])
-        each(along, lambda s: out_copy(c, s).wait())
 
     each(chunks, drain)
     for side, sends in enumerate((gx < across - 1, gx > 0)):
@@ -699,29 +726,28 @@
     fhi, flo = two_parts(mats)
     thi, tlo = two_parts(np.swapaxes(mats, 1, 2))
     ky = jnp.asarray(wave.reshape(count, width), jnp.float32)
-    kx = jnp.asarray(wave[:, :, None], jnp.float32)
     lines = pltpu.VMEM((nvec, along, rows, by), jnp.float32)
     packed = pltpu.VMEM((nvec, count, rows, width), jnp.float32)
     chunks = nvec * CUTS
     levels, labels = heat.reshape(-1, bx, by), labels.reshape(-1, bx, by)
 
-    def trio(tall, wide):
+    def trio(copies, tall, wide):
         kinds = ((nvec, jnp.float32), (3, jnp.float32), (4, jnp.int32))
-        return tuple(pltpu.VMEM((2, depth, tall, wide), kind) for depth, kind in kinds)
+        return tuple(pltpu.VMEM(copies + (depth, tall, wide), kind) for depth, kind in kinds)
 
     dma = pltpu.SemaphoreType.DMA
     anywhere, inside = pl.BlockSpec(memory_space=pl.ANY), pl.BlockSpec(memory_space=pltpu.VMEM)
     return pl.pallas_call(
         whole_kernel,
-        in_specs=[anywhere] * 7 + [inside] * 2,
-        out_specs=anywhere,
-        out_shape=jax.ShapeDtypeStruct(q.shape, jnp.float32),
+        in_specs=[anywhere] * 7 + [inside],
+        out_specs=inside,
+        out_shape=pltpu.VMEM(q.shape, jnp.float32),
         scratch_shapes=[
             lines, packed, packed, packed, lines, pltpu.VMEM((4,) + mats.shape, jnp.bfloat16),
-            pltpu.VMEM(q.shape, jnp.float32), trio(RIM, by), trio(bx, 128),
+            trio((2,), RIM, by), trio((), bx, 128),
             pltpu.VMEM((4, bx + 2 * RIM, 128), jnp.float32),
-            trio(STRIP + 2 * RIM, by),
-            dma((4,)), dma((nvec,)), dma((chunks, along)), dma((chunks,)), dma((chunks,)),
+            trio((2,), STRIP + 2 * RIM, by),
+            dma((4,)), dma((nvec,)), dma((chunks,)), dma((chunks,)),
             dma((nvec,)), dma((nvec,)), dma((chunks,)), dma((chunks,)), dma((chunks,)),
             dma((chunks,)), dma((2, 3)), dma((2, 3)), dma((2, 3)), dma((2,)), dma((2,)), dma((2, 3)),
         ],
@@ -730,11 +756,11 @@
         ),
         cost_estimate=cost(36 * mats.size * nvec * bx * by // length, 64 * nvec * bx * by),
         name="whole",
-    )(q, levels, labels, fhi, flo, thi, tlo, ky, kx)
+    )(q, levels, labels, fhi, flo, thi, tlo, ky)
 
 
 RIM = 8
-VMEM_BYTES = 60 * 2**20
+VMEM_BYTES = 52 * 2**20
 
 
 STRIP = 32
@@ -785,7 +811,9 @@
     along, across = lax.axis_size("gy"), lax.axis_size("gx")
     rows, width = bx // along, by // across
     square = bx * across == by * along
-    if not square or rows % 16 or width % 128 or by % (by * along // OUTER) or bx % (STRIP * nvec):
+    split = nvec == 2 and rows % (16 * CUTS) == 0 and width % 128 == 0 and bx % 64 == 0
+    early = bx // STRIP <= BACK_AT + LAG - STRIPS_AT
+    if not (square and split and early) or by % (by * along // OUTER):
         return shards_general(q, heat, labels)
     return whole(q, heat, labels)
 

time: 221 us -> 206 us (0.932)
  Pallas kernels: 214 us -> 204 us
  local copies, waits for them, and re-layouts: 4.79 us -> 2.02 us
    pallas_call x1, Pallas kernels: 214 us -> 204 us  [whole(): pl.pallas_call(whole_kernel, in_specs=[anywhere] * 7 + [inside], out_spec...]
    unnamed x1, local copies, waits for them, and re-layouts: 4.79 us -> 2.02 us
where the time goes in v3:
time: 206 us
  Pallas kernels  204 us (99%)
    pallas_call x1, Pallas kernels, whole(): pl.pallas_call(whole_kernel, in_specs=[anywhere] * 7 + [inside], out_spec...  204 us

profile of v3, /device:TPU:13, one launch (start us, length us, event | category | flops | bytes accessed | tf_op | source)
XLA Modules:
  0.0 206.0 jit_solution(11862342475028048672)
XLA Ops:
  0.0 204.0 %whole.1 = f32[2,512,1024]{2,1,0:T(8,128)S(1)} custom-call(f32[2,512,1024]{2,1,0:T(8,128)} %q_ref.1, f32[4,512,1024]{2,1,0:T(8,128)} %bitcast.2, s32[4,512,1024]{2,1,0:T(8,128)} %bitcast.3, bf16[8,512,512]{2,1,0:T(8,128)(2,1)} %constant.11.clone.fhi_ref, bf16[8,512,512]{2,1,0:T(8,128)(2,1)} %constant.12.clone.flo_ref, ...), custom_call_target="tpu_custom_call" | custom-call | flops 19327352832 | bytes 67108864 | tf_op jit(solution)/shard_map/whole/pallas_call | solution.py:740
  204.0 2.0 copy.10
